TPU v7x, 128 devices: a whole 4x4x4 slice. The times are simulated.
128 devices in a mesh: seq: 8 (over y_hi, x), res: 16 (over z, y_lo, core).
Axes of the slice: x: 4, y: 4 (y_hi: 2, y_lo: 2; y = y_hi * 2 + y_lo), z: 4, core: 2. Of those that a mesh axis runs over, the one named last changes fastest.
Arguments:
- homolog_tensor: bfloat16 [128, 2048, 256], P('seq', 'res'), may hold values from -3 to 3
- horizontal_probe_matrix: bfloat16 [256, 256], replicated, may hold values from -3 to 3, as said below
- horizontal_lookup_matrix: bfloat16 [256, 256], replicated, may hold values from -3 to 3, as said below
- horizontal_payload_matrix: bfloat16 [256, 256], replicated, may hold values from -0.375 to 0.375
- horizontal_sigmoid_matrix: bfloat16 [256, 256], replicated, may hold values from -0.375 to 0.375
- horizontal_final_matrix: bfloat16 [256, 256], replicated, may hold values from -0.375 to 0.375
- vertical_probe_matrix: bfloat16 [256, 256], replicated, may hold values from -3 to 3, as said below
- vertical_lookup_matrix: bfloat16 [256, 256], replicated, may hold values from -3 to 3, as said below
- vertical_payload_matrix: bfloat16 [256, 256], replicated, may hold values from -0.375 to 0.375
- vertical_sigmoid_matrix: bfloat16 [256, 256], replicated, may hold values from -0.375 to 0.375
- vertical_final_matrix: bfloat16 [256, 256], replicated, may hold values from -0.375 to 0.375
- expanding_matrix: bfloat16 [256, 1024], replicated, may hold values from -0.375 to 0.375
- shrinking_matrix: bfloat16 [1024, 256], replicated, may hold values from -0.1875 to 0.1875
Outputs:
- refreshed_homologs: bfloat16 [128, 2048, 256], P('seq', 'res')
Inputs may be any that keep to these rules, and one draw needn't show every extreme that they name: `horizontal_probe_matrix`: entries of a projection matrix. `horizontal_lookup_matrix`: entries of a projection matrix. `vertical_probe_matrix`: entries of a projection matrix. `vertical_lookup_matrix`: entries of a projection matrix.
All inputs are finite; a program needn't handle non-finite values.
Results may differ from a plain program's by a relative error of at most 0.023.
Values may be sent and summed in bfloat16 or wider, within the bound.
A program may use at most 128 MiB of HBM per device.

v0:
```python
import math

import jax
import jax.numpy as jnp
from jax import lax
from jax.sharding import PartitionSpec as P

HEADS = 8
HEAD_DIM = 32


def layer_normalize(sample_entries):
    center = sample_entries - jnp.mean(sample_entries, axis=-1, keepdims=True)
    spread = jnp.mean(center * center, axis=-1, keepdims=True)
    return center * lax.rsqrt(spread + 1e-05)


def softmax_last(sample_entries):
    highest = jnp.max(sample_entries, axis=-1, keepdims=True)
    expo = jnp.exp(sample_entries - highest)
    return expo / jnp.sum(expo, axis=-1, keepdims=True)


def linear_project(inputs, weight):
    return jnp.dot(inputs, weight, preferred_element_type=jnp.float32)


def on_device(
    homolog_tensor,
    horizontal_probe_matrix,
    horizontal_lookup_matrix,
    horizontal_payload_matrix,
    horizontal_sigmoid_matrix,
    horizontal_final_matrix,
    vertical_probe_matrix,
    vertical_lookup_matrix,
    vertical_payload_matrix,
    vertical_sigmoid_matrix,
    vertical_final_matrix,
    expanding_matrix,
    shrinking_matrix,
):
    homolog_partition, position_partition, feature_depth = homolog_tensor.shape
    groups = lax.axis_size("seq")
    total_seqs = homolog_partition * groups
    merged_homologs = homolog_tensor.astype(jnp.float32).reshape(
        homolog_partition * position_partition, feature_depth
    )
    normalized_input = layer_normalize(merged_homologs).astype(jnp.bfloat16)
    query_rows = (
        linear_project(normalized_input, horizontal_probe_matrix)
        .astype(jnp.bfloat16)
        .reshape(homolog_partition, position_partition, HEADS, HEAD_DIM)
    )
    key_rows = (
        linear_project(normalized_input, horizontal_lookup_matrix)
        .astype(jnp.bfloat16)
        .reshape(homolog_partition, position_partition, feature_depth)
    )
    value_local = (
        linear_project(normalized_input, horizontal_payload_matrix)
        .astype(jnp.bfloat16)
        .reshape(homolog_partition, position_partition, feature_depth)
    )
    row_gates = jax.nn.sigmoid(linear_project(normalized_input, horizontal_sigmoid_matrix))
    score_scale = 1.0 / math.sqrt(total_seqs * HEAD_DIM)
    key_piece = lax.all_gather(key_rows, "res", axis=1, tiled=True)
    split_keys = key_piece.reshape(homolog_partition, key_piece.shape[1], HEADS, HEAD_DIM)
    partial_logits = jnp.einsum(
        "sihd,sjhd->hij", query_rows, split_keys, preferred_element_type=jnp.float32
    )
    tied = lax.psum(partial_logits, "seq")
    row_weights = softmax_last(tied * score_scale).astype(jnp.bfloat16)
    value_piece = lax.all_gather(value_local, "res", axis=1, tiled=True)
    count = value_piece.shape[1]
    split_values = value_piece.reshape(homolog_partition, count, HEADS, HEAD_DIM)
    term = jnp.einsum(
        "pmn,qnpc->qmpc", row_weights, split_values, preferred_element_type=jnp.float32
    )
    attended = term.reshape(homolog_partition, position_partition, feature_depth)
    attended = attended.reshape(homolog_partition * position_partition, feature_depth)
    row_attention_update = (row_gates * attended).astype(jnp.bfloat16)
    row_updated = (
        merged_homologs + linear_project(row_attention_update, horizontal_final_matrix)
    ).astype(jnp.bfloat16)
    blocked = row_updated.reshape(
        homolog_partition, groups, position_partition // groups, feature_depth
    )
    columns = lax.all_to_all(blocked, "seq", split_axis=1, concat_axis=0, tiled=True)
    rows_in = columns.reshape(total_seqs, columns.shape[2], feature_depth)
    count = rows_in.shape[1]
    rows_flat = rows_in.astype(jnp.float32).reshape(total_seqs * count, feature_depth)
    normed_col = layer_normalize(rows_flat).astype(jnp.bfloat16)
    query_col = (
        linear_project(normed_col, vertical_probe_matrix)
        .astype(jnp.bfloat16)
        .reshape(total_seqs, count, HEADS, HEAD_DIM)
    )
    key_col = (
        linear_project(normed_col, vertical_lookup_matrix)
        .astype(jnp.bfloat16)
        .reshape(total_seqs, count, HEADS, HEAD_DIM)
    )
    value_col = (
        linear_project(normed_col, vertical_payload_matrix)
        .astype(jnp.bfloat16)
        .reshape(total_seqs, count, HEADS, HEAD_DIM)
    )
    gate_col = jax.nn.sigmoid(linear_project(normed_col, vertical_sigmoid_matrix))
    scores = jnp.einsum("snhd,tnhd->nhst", query_col, key_col, preferred_element_type=jnp.float32)
    weights_col = softmax_last(scores * (1.0 / math.sqrt(HEAD_DIM))).astype(jnp.bfloat16)
    mixed = jnp.einsum(
        "kmpv,vkml->pkml", weights_col, value_col, preferred_element_type=jnp.float32
    )
    update_col = (gate_col * mixed.reshape(total_seqs * count, feature_depth)).astype(jnp.bfloat16)
    result = (rows_flat + linear_project(update_col, vertical_final_matrix)).astype(jnp.bfloat16)
    finished = result.reshape(total_seqs, count, feature_depth)
    restored = lax.all_to_all(
        finished.reshape(total_seqs, 1, finished.shape[1], feature_depth),
        "seq",
        split_axis=0,
        concat_axis=1,
        tiled=True,
    )
    column_updated = restored.reshape(homolog_partition * position_partition, feature_depth).astype(
        jnp.float32
    )
    normed_tr = layer_normalize(column_updated).astype(jnp.bfloat16)
    hidden_state = jax.nn.relu(linear_project(normed_tr, expanding_matrix)).astype(jnp.bfloat16)
    refreshed_homologs = (column_updated + linear_project(hidden_state, shrinking_matrix)).astype(
        jnp.bfloat16
    )
    return refreshed_homologs.reshape(homolog_partition, position_partition, feature_depth)


def solution(mesh):
    in_specs = (P("seq", "res", None), P(), P(), P(), P(), P(), P(), P(), P(), P(), P(), P(), P())
    out_specs = P("seq", "res", None)
    return jax.shard_map(
        on_device, mesh=mesh, in_specs=in_specs, out_specs=out_specs, check_vma=False
    )
```

profile of v0, /device:TPU:0, one launch (start us, length us, event | category | flops | bytes accessed | tf_op | source)
XLA Modules:
  0.0 570.3 jit_solution(4093201901602135783)
XLA Ops:
  6.5 1.7 convert_reduce_fusion
  8.3 1.9 multiply_reduce_fusion.2
  10.9 1.4 convolution_convert_fusion.3
  12.3 2.3 copy.39
  16.1 2.3 copy.38
  18.4 2.4 copy.62
  20.8 95.9 %all-gather.5.cloned.1.call-done = bf16[16,2048,256]{1,2,0:T(8,128)(2,1)} async-done(((bf16[16,128,256]{1,2,0:T(8,128)(2,1)}), bf16[16,2048,256]{1,2,0:T(8,128)(2,1)}) %all-gather.5.cloned.1.call-update) | async-done | bytes 16777232 | tf_op jit(solution)/shard_map/all_gather | solution.py:67
  116.7 19.6 %fusion.12 = f32[8,128,2048]{2,1,0:T(8,128)} fusion(bf16[16,128,8,32]{1,0,3,2:T(8,128)(2,1)} %bitcast.114, bf16[16,2048,8,32]{1,3,2,0:T(8,128)(2,1)} %bitcast.109), kind=kOutput, calls=%fused_computation.15 | convolution fusion | flops 2147483648 | bytes 26214400 | tf_op jit(solution)/shard_map/sihd,sjhd->hij/dot_general | solution.py:69
  138.7 2.3 copy.37
  141.0 181.1 %all-reduce.2.cloned.1.call-done = f32[8,128,2048]{2,1,0:T(8,128)} async-done(((f32[8,128,2048]{2,1,0:T(8,128)}), f32[8,128,2048]{2,1,0:T(8,128)}) %all-reduce.2.cloned.1.call-update) | async-done | bytes 8388624 | tf_op jit(solution)/shard_map/psum | solution.py:72
  322.1 10.9 %fusion.64 = (f32[8,128]{1,0:T(8,128)S(1)}, f32[8,128,2048]{2,1,0:T(8,128)}) fusion(f32[8,128,2048]{2,1,0:T(8,128)} %all-reduce.2.cloned.1.call-done), kind=kOutput, calls=%fused_computation.87 | output fusion | flops 8390655 | bytes 16781312 | tf_op jit(solution)/shard_map/sub | solution.py:20
  333.0 87.7 %all-gather.3.cloned.1.call-done = bf16[16,2048,256]{1,2,0:T(8,128)(2,1)} async-done(((bf16[16,128,256]{1,2,0:T(8,128)(2,1)}), bf16[16,2048,256]{1,2,0:T(8,128)(2,1)}) %all-gather.3.cloned.1.call-update) | async-done | bytes 16777232 | tf_op jit(solution)/shard_map/all_gather | solution.py:74
  420.7 10.6 %fusion.49 = f32[16,128,8,32]{1,3,0,2:T(8,128)S(1)} fusion(f32[8,128,2048]{2,1,0:T(8,128)} %get-tuple-element.8, f32[8,128]{1,0:T(8,128)S(1)} %get-tuple-element.7, bf16[16,2048,8,32]{1,3,2,0:T(8,128)(2,1)} %bitcast.121), kind=kOutput, calls=%fused_computation.68 | convolution fusion | flops 2151677952 | bytes 27267072 | tf_op jit(solution)/shard_map/pmn,qnpc->qmpc/dot_general | solution.py:77
  432.5 2.2 copy.89
  434.7 2.9 copy.43
  437.7 3.4 fusion.32
  442.4 24.1 %all_to_all.8 = bf16[16,8,16,256]{3,2,0,1:T(8,128)(2,1)S(1)} all-to-all(bf16[16,8,16,256]{3,2,0,1:T(8,128)(2,1)S(1)} %copy.44), channel_id=1, replica_groups=mesh['seq'=8,'res'=16] {'seq'}, dimensions={1} | all-to-all | bytes 2097152 | tf_op jit(solution)/shard_map/all_to_all | solution.py:89
  471.3 1.4 convolution_convert_fusion.2
  472.8 5.8 %reshape.173 = bf16[128,16,8,32]{3,2,1,0:T(8,128)(2,1)} reshape(bf16[2048,256]{1,0:T(8,128)(2,1)} %convolution_convert_fusion.2) | data formatting | bytes 2097152 | tf_op jit(solution)/shard_map/reshape | solution.py:107
  478.5 5.8 %reshape.174 = bf16[128,16,8,32]{3,2,1,0:T(8,128)(2,1)} reshape(bf16[2048,256]{1,0:T(8,128)(2,1)} %convolution_convert_fusion.1) | data formatting | bytes 2097152 | tf_op jit(solution)/shard_map/reshape | solution.py:97
  484.3 5.8 %reshape.175 = bf16[128,16,8,32]{3,2,1,0:T(8,128)(2,1)} reshape(bf16[2048,256]{1,0:T(8,128)(2,1)} %convolution_convert_fusion) | data formatting | bytes 2097152 | tf_op jit(solution)/shard_map/reshape | solution.py:102
  490.1 9.0 %fusion.18 = f32[16,8,128,128]{2,3,1,0:T(8,128)S(1)} fusion(bf16[128,16,8,32]{3,2,1,0:T(8,128)(2,1)} %reshape.175, bf16[128,16,8,32]{3,2,1,0:T(8,128)(2,1)} %reshape.174), kind=kOutput, calls=%fused_computation.19 | convolution fusion | flops 134217728 | bytes 10485760 | tf_op jit(solution)/shard_map/snhd,tnhd->nhst/dot_general | solution.py:110
  499.1 4.5 fusion.65
  503.6 7.7 %fusion.46 = f32[128,16,8,32]{0,3,2,1:T(8,128)} fusion(f32[16,8,128,128]{2,3,1,0:T(8,128)} %get-tuple-element.10, f32[16,8,128]{2,1,0:T(8,128)S(1)} %get-tuple-element.9, bf16[128,16,8,32]{3,2,1,0:T(8,128)(2,1)S(1)} %copy-done.3), kind=kOutput, calls=%fused_computation.67 | convolution fusion | flops 138412032 | bytes 11599872 | tf_op jit(solution)/shard_map/kmpv,vkml->pkml/dot_general | solution.py:112
  511.2 8.4 %copy.54 = f32[128,16,8,32]{3,2,1,0:T(8,128)} copy(f32[128,16,8,32]{0,3,2,1:T(8,128)} %fusion.46) | data formatting | bytes 4194304 | tf_op jit(solution)/shard_map/kmpv,vkml->pkml/transpose | solution.py:112
  519.6 7.0 %reshape.176 = f32[2048,256]{1,0:T(8,128)} reshape(f32[128,16,8,32]{3,2,1,0:T(8,128)} %copy.54) | data formatting | bytes 4194304 | tf_op jit(solution)/shard_map/reshape | solution.py:115
  526.6 1.6 bitcast_convert_fusion
  528.3 4.0 fusion.33
  532.3 20.8 %all_to_all.9 = bf16[128,1,16,256]{3,2,1,0:T(8,128)(2,1)S(1)} all-to-all(bf16[128,1,16,256]{3,2,1,0:T(8,128)(2,1)} %bitcast.119), channel_id=1, replica_groups=mesh['seq'=8,'res'=16] {'seq'}, dimensions={0} | all-to-all | bytes 2097152 | tf_op jit(solution)/shard_map/all_to_all | solution.py:118
  554.2 1.7 copy.56
  556.0 2.9 fusion.37
  558.9 4.7 fusion.31
  (60 shorter events, 13.0 us)
Async XLA Ops:
  6.5 552.4 %copy-start = (bf16[1024,256]{1,0:T(8,128)(2,1)S(1)}, bf16[1024,256]{1,0:T(8,128)(2,1)}, u32[]{:S(2)}) copy-start(bf16[1024,256]{1,0:T(8,128)(2,1)} %param.25) | copy-start | bytes 1572868
  6.5 3.6 copy-start.1
  6.5 4.3 copy-start.4
  6.5 110.2 %all-gather.5.cloned.1.call-start = ((), (), s32[]{:S(2)}) async-start(), calls=%async_computation.3 | async-start | bytes 17825792 | tf_op jit(solution)/shard_map/all_gather | solution.py:67
  12.3 2.4 copy-start.5
  14.6 307.4 %all-reduce.2.cloned.1.call-start = ((), (), s32[]{:S(2)}) async-start(), calls=%async_computation.4 | async-start | bytes 16777216 | tf_op jit(solution)/shard_map/psum | solution.py:72
  136.3 0.9 copy-start.6
  136.4 284.3 %all-gather.3.cloned.1.call-start = ((), (), s32[]{:S(2)}) async-start(), calls=%async_computation.2 | async-start | bytes 17825792 | tf_op jit(solution)/shard_map/all_gather | solution.py:74
  434.7 2.9 copy-start.11
  434.7 2.9 copy-start.12
  466.8 1.7 copy-start.7
  467.8 2.2 copy-start.8
  468.5 2.8 copy-start.9
  499.1 4.5 copy-start.3
  526.6 1.7 copy-start.13
  526.6 1.7 copy-start.14
  555.9 3.0 copy-start.2
  555.9 3.0 copy-start.10
Sparse Core Ops, SparseCore 0:
  14.8 101.9 all-gather.4
  136.5 185.5 all-reduce.1
  323.7 96.9 all-gather.2
where the time goes:
time: 580 us; the launch traced here: 570 us
  waiting for transfers between devices  365 us (63%)
  matrix products  67.5 us (12%)
  local copies, waits for them, and re-layouts  52.1 us (9%)
  blocking collectives  44.9 us (8%)
  other arithmetic  27 us (5%)
  between operations  13.6 us (2%)
    psum x1, waiting for transfers between devices, on_device(): tied = lax.psum(partial_logits, 'seq')  181 us
    all_gather x1, waiting for transfers between devices, on_device(): key_piece = lax.all_gather(key_rows, 'res', axis=1, tiled=True)  95.9 us
    all_gather x1, waiting for transfers between devices, on_device(): value_piece = lax.all_gather(value_local, 'res', axis=1, tiled=True)  87.7 us
    all_to_all x1, blocking collectives, on_device(): lax.all_to_all(blocked, 'seq', split_axis=1, concat_axis=0, tiled=True)  24.1 us
    all_to_all x1, blocking collectives, on_device(): lax.all_to_all(finished.reshape(total_seqs, 1, finished.shape[1], feature...  20.8 us
    dot_general x9, matrix products, linear_project(): return jnp.dot(inputs, weight, preferred_element_type=jnp.float32)  20.6 us
    dot_general x1, matrix products, on_device(): jnp.einsum('sihd,sjhd->hij', query_rows, split_keys, preferred_element_ty...  19.6 us
    sub x2, other arithmetic, softmax_last(): expo = jnp.exp(sample_entries - highest)  15.4 us
  transfers between devices with their start and end apart: 3, of which 3 were waited for; matrix products, arithmetic and copies ran while one was open for 4% of the time, Pallas kernels for 0%

commit v1 on v0

v1 whole, which is shorter than its diff:
```python
import math

import jax
import jax.numpy as jnp
from jax import lax
from jax.experimental import pallas as pl
from jax.experimental.pallas import tpu as pltpu
from jax.sharding import PartitionSpec as P

HEADS = 8
HEAD_DIM = 32
SEQ_DEVICES = 8
MESH = pl.DeviceIdType.MESH
BF16 = jnp.bfloat16
F32 = jnp.float32
NT = (((1,), (1,)), ((), ()))


def layer_normalize(entries):
    center = entries - jnp.mean(entries, axis=-1, keepdims=True)
    spread = jnp.mean(center * center, axis=-1, keepdims=True)
    return center * lax.rsqrt(spread + 1e-05)


def matmul(a, b):
    return jnp.dot(a, b, preferred_element_type=F32)


def matmul_nt(a, b):
    return lax.dot_general(a, b, NT, preferred_element_type=F32)


def flip(a):
    return a.astype(F32).T.astype(BF16)


def remote(src, dst, send, recv, device):
    return pltpu.make_async_remote_copy(
        src_ref=src, dst_ref=dst, send_sem=send, recv_sem=recv, device_id=device, device_id_type=MESH
    )


def row_kernel(
    x, wq, wk, wv, wg, wf, out,
    normed, wt, ks, qs, vs, kz, vz, qg, logits, probs, gates, stats,
    o_part, oc_s, oc_r, oy_s, oy_r, oa_s, ob, after,
    ka_s, ka_r, qa_s, qa_r, va_s, va_r, kz_s, kz_r, vz_s, vz_r, qp_s, qp_r,
    st_s, st_r, oc_ss, oc_rs, oy_ss, oy_rs, oa_ss, oa_rs, col_s, col_r, own_s,
):
    me = lax.axis_index("seq")
    res = lax.axis_index("res")
    z = res // 4
    yl = lax.rem(res // 2, 2)
    c = lax.rem(res, 2)
    here = lax.rem(res, 4)

    def at_res(zz, yy, cc):
        return (me, zz * 4 + yy * 2 + cc)

    z_up = lax.rem(z + 1, 4)
    z_down = lax.rem(z + 3, 4)
    z_far = lax.rem(z + 2, 4)
    up = at_res(z_up, yl, c)
    down = at_res(z_down, yl, c)
    twin = at_res(z, yl, 1 - c)
    beside = at_res(z, 1 - yl, c)
    across = at_res(z, 1 - yl, 1 - c)

    def ahead(t):
        return lax.rem(me + t, SEQ_DEVICES)

    def behind(t):
        return lax.rem(me + SEQ_DEVICES - t, SEQ_DEVICES)

    barrier = pltpu.get_barrier_semaphore()
    partners = [(ahead(t), res) for t in range(1, SEQ_DEVICES)] + [up, down, twin, beside, across]
    for device in partners:
        pl.semaphore_signal(barrier, inc=1, device_id=device, device_id_type=MESH)
    pl.semaphore_wait(barrier, len(partners))

    wt[0:256, :] = flip(wk[...])
    wt[256:512, :] = flip(wq[...])
    wt[512:768, :] = flip(wv[...])
    wt[768:1024, :] = flip(wg[...])
    logits[...] = jnp.zeros_like(logits)

    @pl.loop(0, 4)
    def _(quad):
        rows = pl.ds(pl.multiple_of(quad * 512, 512), 512)
        part = layer_normalize(x[rows, :].astype(F32)).astype(BF16)
        normed[rows, :] = part
        keys = matmul_nt(wt[0:256, :], part)
        lanes = pl.ds(pl.multiple_of(quad * 128, 128), 128)
        for h in range(HEADS):
            block = keys[32 * h : 32 * h + 32, :]
            stack = jnp.concatenate([block[:, 128 * s : 128 * s + 128] for s in range(4)], axis=0)
            ks[h, :, lanes] = stack.T.astype(BF16)

    def ka(t):
        return remote(ks.at[behind(t)], kz.at[z, me], ka_s.at[t], ka_r.at[t], (behind(t), res))

    def qa(t):
        return remote(qs.at[behind(t)], qg.at[here, me], qa_s.at[t], qa_r.at[t], (behind(t), res))

    def va(t):
        return remote(vs.at[behind(t)], vz.at[z, me], va_s.at[t], va_r.at[t], (behind(t), res))

    own_k = pltpu.make_async_copy(ks.at[me], kz.at[z, me], own_s.at[0])
    own_q = pltpu.make_async_copy(qs.at[me], qg.at[here, me], own_s.at[1])
    own_v = pltpu.make_async_copy(vs.at[me], vz.at[z, me], own_s.at[2])
    own_k.start()
    for t in range(1, SEQ_DEVICES):
        ka(t).start()

    @pl.loop(0, 4)
    def _(quad):
        rows = pl.ds(pl.multiple_of(quad * 512, 512), 512)
        both = matmul_nt(wt[256:768, :], normed[rows, :]).astype(BF16)
        for h in range(HEADS):
            for s in range(4):
                place = pl.ds(pl.multiple_of(quad * 128 + 32 * s, 32), 32)
                lanes = slice(128 * s, 128 * s + 128)
                qs[h, place, :] = both[32 * h : 32 * h + 32, lanes]
                vs[h, place, :] = both[256 + 32 * h : 256 + 32 * h + 32, lanes]

    own_q.start()
    own_v.start()

    def ring(buf, send, recv, t):
        g = ahead(t)
        return (
            remote(buf.at[z, g], buf.at[z, g], send.at[0, t], recv.at[0, t], up),
            remote(buf.at[z, g], buf.at[z, g], send.at[1, t], recv.at[1, t], down),
        )

    def ring_arrived(buf, send, recv, t):
        g = ahead(t)
        remote(buf.at[z_down, g], buf.at[z_down, g], send.at[0, t], recv.at[0, t], up).wait_recv()
        remote(buf.at[z_up, g], buf.at[z_up, g], send.at[1, t], recv.at[1, t], down).wait_recv()

    def onward_up(buf, send, recv, t):
        g = ahead(t)
        return remote(buf.at[z_down, g], buf.at[z_down, g], send.at[2, t], recv.at[2, t], up)

    def onward_down(buf, send, recv, t):
        g = ahead(t)
        return remote(buf.at[z_up, g], buf.at[z_up, g], send.at[2, t], recv.at[2, t], down)

    def far_arrived(buf, send, recv, t):
        g = ahead(t)
        remote(buf.at[z_far, g], buf.at[z_far, g], send.at[2, t], recv.at[2, t], up).wait_recv()

    def ring_forward(buf, send, recv, t):
        ring_arrived(buf, send, recv, t)

        @pl.when(lax.rem(t, 2) == 0)
        def _():
            onward_up(buf, send, recv, t).start()

        @pl.when(lax.rem(t, 2) == 1)
        def _():
            onward_down(buf, send, recv, t).start()

    kzs = (kz, kz_s, kz_r)
    vzs = (vz, vz_s, vz_r)

    here_twin = yl * 2 + (1 - c)
    here_beside = (1 - yl) * 2 + c
    here_across = (1 - yl) * 2 + (1 - c)

    def q_twin(t):
        g = ahead(t)
        return remote(qg.at[here, g], qg.at[here, g], qp_s.at[0, t], qp_r.at[0, t], twin)

    def q_beside(t):
        g = ahead(t)
        return remote(qg.at[here, g], qg.at[here, g], qp_s.at[1, t], qp_r.at[1, t], beside)

    def q_onward(t):
        g = ahead(t)
        return remote(qg.at[here_beside, g], qg.at[here_beside, g], qp_s.at[2, t], qp_r.at[2, t], twin)

    def q_arrived(slot, place, t):
        g = ahead(t)
        remote(qg.at[place, g], qg.at[place, g], qp_s.at[slot, t], qp_r.at[slot, t], twin).wait_recv()

    def add_logits(t):
        g = ahead(t)
        queries = jnp.concatenate([qg[p, g] for p in range(4)], axis=1)
        for zz in range(4):
            logits[128 * zz : 128 * zz + 128, :] += matmul(kz[zz, g], queries)

    scale = 1.0 / math.sqrt(SEQ_DEVICES * 16 * HEAD_DIM)

    def stat_copy(i, device):
        return remote(stats.at[here], stats.at[here], st_s.at[i], st_r.at[i], device)

    def stat_wait(i, place):
        remote(stats.at[place], stats.at[place], st_s.at[i], st_r.at[i], twin).wait_recv()

    def local_softmax():
        highest = jnp.max(logits[...], axis=0, keepdims=True)
        total = jnp.zeros((1, 512), F32)
        for zz in range(4):
            rows = slice(128 * zz, 128 * zz + 128)
            expo = jnp.exp((logits[rows, :] - highest) * scale)
            logits[rows, :] = expo
            total += jnp.sum(expo, axis=0, keepdims=True)
        stats[here, 0] = jnp.broadcast_to(highest, (8, 512))
        stats[here, 1] = jnp.broadcast_to(total, (8, 512))
        stat_copy(0, twin).start()
        stat_copy(1, beside).start()
        stat_copy(2, across).start()

    def finish_softmax():
        stat_wait(0, here_twin)
        stat_wait(1, here_beside)
        stat_wait(2, here_across)
        highest = stats[0, 0]
        for p in range(1, 4):
            highest = jnp.maximum(highest, stats[p, 0])
        total = jnp.zeros((8, 512), F32)
        for p in range(4):
            total += stats[p, 1] * jnp.exp((stats[p, 0] - highest) * scale)
        factor = jnp.exp((stats[here, 0] - highest) * scale) / total
        factor = factor[0:1, :]
        for zz in range(4):
            rows = slice(128 * zz, 128 * zz + 128)
            probs[rows, :] = (logits[rows, :] * factor).astype(BF16)

    def oc(t):
        return remote(oc_s.at[t], oc_r.at[t], oc_ss.at[t], oc_rs.at[t], twin)

    def oy(t):
        return remote(oy_s.at[t], oy_r.at[t], oy_ss.at[t], oy_rs.at[t], beside)

    def oa(t):
        return remote(oa_s.at[t], ob.at[me], oa_ss.at[t], oa_rs.at[t], (ahead(t), res))

    def attend(t):
        g = ahead(t)
        slot = lax.rem(t, 2)

        @pl.loop(0, 4)
        def _(rb):
            rows = pl.ds(pl.multiple_of(rb * 128, 128), 128)
            values = jnp.concatenate([vz[zz, g, rows, :] for zz in range(4)], axis=1)
            term = matmul(values, probs[...])
            for p in range(4):
                o_part[slot, p, rows, :] = term[:, 128 * p : 128 * p + 128]

        for y in range(2):
            oc_s[t, y] = o_part[slot, 2 * y + 1 - c].astype(BF16)
        oc(t).start()

    def add_twin(t):
        slot = lax.rem(t, 2)
        oc(t).wait_recv()
        oy_s[t] = (o_part[slot, here_beside] + oc_r[t, 1 - yl].astype(F32)).astype(BF16)
        oy(t).start()

    def add_beside(t):
        slot = lax.rem(t, 2)
        oy(t).wait_recv()
        total = o_part[slot, here] + oc_r[t, yl].astype(F32) + oy_r[t].astype(F32)

        @pl.when(t == 0)
        def _():
            ob[me] = total.astype(BF16)

        @pl.when(t > 0)
        def _():
            oa_s[t] = total.astype(BF16)
            oa(t).start()

    def gate_quad(quad):
        rows = pl.ds(pl.multiple_of(quad * 512, 512), 512)
        gate = jax.nn.sigmoid(matmul_nt(wt[768:1024, :], normed[rows, :]))
        for s in range(4):
            gates[quad * 4 + s] = gate[:, 128 * s : 128 * s + 128]

    @pl.loop(0, 24)
    def _(tick):
        def during(first, action, count=8):
            @pl.when((tick >= first) & (tick < first + count))
            def _():
                action(tick - first)

        def k_own(t):
            @pl.when(t == 0)
            def _():
                own_k.wait()

            @pl.when(t > 0)
            def _():
                remote(ks.at[0], kz.at[z, ahead(t)], ka_s.at[t], ka_r.at[t], (behind(t), res)).wait_recv()
                qa(t).start()

            for copy in ring(*kzs, t):
                copy.start()

        def q_peers(t):
            @pl.when(t == 0)
            def _():
                own_q.wait()

            @pl.when(t > 0)
            def _():
                remote(qs.at[0], qg.at[here, ahead(t)], qa_s.at[t], qa_r.at[t], (behind(t), res)).wait_recv()

            q_twin(t).start()
            q_beside(t).start()

        def q_forward(t):
            q_arrived(1, here_beside, t)
            q_onward(t).start()

        def v_send(t):
            @pl.when(t > 0)
            def _():
                va(t).start()

        def v_own(t):
            @pl.when(t == 0)
            def _():
                own_v.wait()

            @pl.when(t > 0)
            def _():
                remote(vs.at[0], vz.at[z, ahead(t)], va_s.at[t], va_r.at[t], (behind(t), res)).wait_recv()

            for copy in ring(*vzs, t):
                copy.start()

        def add_chunk(t):
            far_arrived(*kzs, t)
            q_arrived(0, here_twin, t)
            q_arrived(2, here_across, t)
            add_logits(t)

        def attend_chunk(t):
            far_arrived(*vzs, t)
            attend(t)

        during(16, add_beside)
        during(15, add_twin)
        during(0, k_own)
        during(8, v_own)
        during(2, lambda t: ring_forward(*kzs, t))
        during(10, lambda t: ring_forward(*vzs, t))
        during(2, q_peers)
        during(4, q_forward)
        during(3, v_send)
        during(3, gate_quad, 4)
        during(5, add_chunk)
        during(13, lambda t: local_softmax(), 1)
        during(14, lambda t: finish_softmax(), 1)
        during(14, attend_chunk)

    for t in range(1, SEQ_DEVICES):
        remote(oa_s.at[t], ob.at[behind(t)], oa_ss.at[t], oa_rs.at[t], (ahead(t), res)).wait_recv()

    @pl.loop(0, 8)
    def _(pair):
        flipped = []
        for k in range(2):
            s = pair * 2 + k
            rows = pl.ds(pl.multiple_of(s * 32, 32), 32)
            mixed = jnp.concatenate([ob[h, rows, :] for h in range(HEADS)], axis=0).astype(F32)
            flipped.append((gates[s] * mixed).astype(BF16).astype(F32).T.astype(BF16))
        update = jnp.concatenate(flipped, axis=0)
        rows = pl.ds(pl.multiple_of(pair * 256, 256), 256)
        total = x[rows, :].astype(F32) + matmul(update, wf[...])
        total = total.astype(BF16)
        for k in range(2):
            after[pair * 2 + k] = total[128 * k : 128 * k + 128, :]

    def columns(t):
        g = ahead(t)
        return remote(
            after.at[:, pl.ds(pl.multiple_of(g * 16, 16), 16), :],
            out.at[pl.ds(pl.multiple_of(me * 16, 16), 16)],
            col_s.at[t], col_r.at[t], (g, res),
        )

    mine = pl.ds(pl.multiple_of(me * 16, 16), 16)
    own_c = pltpu.make_async_copy(after.at[:, mine, :], out.at[mine], own_s.at[3])
    own_c.start()
    for t in range(1, SEQ_DEVICES):
        columns(t).start()
    own_c.wait()
    for t in range(1, SEQ_DEVICES):
        columns(t).wait_send()
        remote(
            after.at[:, mine, :],
            out.at[pl.ds(pl.multiple_of(behind(t) * 16, 16), 16)],
            col_s.at[t], col_r.at[t], (ahead(t), res),
        ).wait_recv()

    stat_copy(0, twin).wait_send()
    stat_copy(1, beside).wait_send()
    stat_copy(2, across).wait_send()

    @pl.loop(0, 8)
    def _(t):
        @pl.when(t > 0)
        def _():
            ka(t).wait_send()
            qa(t).wait_send()
            va(t).wait_send()
            oa(t).wait_send()

        for buf in (kzs, vzs):
            for copy in ring(*buf, t):
                copy.wait_send()

            @pl.when(lax.rem(t, 2) == 0)
            def _():
                onward_up(*buf, t).wait_send()

            @pl.when(lax.rem(t, 2) == 1)
            def _():
                onward_down(*buf, t).wait_send()

        q_twin(t).wait_send()
        q_beside(t).wait_send()
        q_onward(t).wait_send()
        oc(t).wait_send()
        oy(t).wait_send()


def row_attention(x, wq, wk, wv, wg, wf):
    dma = pltpu.SemaphoreType.DMA
    vmem = pltpu.VMEM
    return pl.pallas_call(
        row_kernel,
        name="row_attention",
        out_shape=jax.ShapeDtypeStruct((128, 16, 256), BF16),
        in_specs=[pl.BlockSpec(memory_space=vmem)] * 6,
        out_specs=pl.BlockSpec(memory_space=vmem),
        scratch_shapes=[
            vmem((2048, 256), BF16),
            vmem((1024, 256), BF16),
            vmem((8, 128, 512), BF16),
            vmem((8, 512, 128), BF16),
            vmem((8, 512, 128), BF16),
            vmem((4, 8, 128, 512), BF16),
            vmem((4, 8, 512, 128), BF16),
            vmem((4, 8, 512, 128), BF16),
            vmem((512, 512), F32),
            vmem((512, 512), BF16),
            vmem((16, 256, 128), F32),
            vmem((4, 2, 8, 512), F32),
            vmem((2, 4, 512, 128), F32),
            vmem((8, 2, 512, 128), BF16),
            vmem((8, 2, 512, 128), BF16),
            vmem((8, 512, 128), BF16),
            vmem((8, 512, 128), BF16),
            vmem((8, 512, 128), BF16),
            vmem((8, 512, 128), BF16),
            vmem((16, 128, 256), BF16),
        ]
        + [dma((8,))] * 6
        + [dma((3, 8))] * 6
        + [dma((3,))] * 2
        + [dma((8,))] * 8
        + [dma((4,))],
        compiler_params=pltpu.CompilerParams(
            collective_id=0, has_side_effects=True, vmem_limit_bytes=60 * 2**20
        ),
    )(x, wq, wk, wv, wg, wf)


def swap_matrix():
    a = lax.broadcasted_iota(jnp.int32, (256, 256), 0)
    b = lax.broadcasted_iota(jnp.int32, (256, 256), 1)
    return jnp.where(b == ((a & 15) << 4) + (a >> 4), 1.0, 0.0).astype(BF16)


def column_kernel(
    xc, wq, wk, wv, wg, wf, we, ws, out,
    swap, x2, wt, wide, done, back, send_sem, recv_sem,
):
    me = lax.axis_index("seq")
    res = lax.axis_index("res")

    def ahead(t):
        return lax.rem(me + t, SEQ_DEVICES)

    def behind(t):
        return lax.rem(me + SEQ_DEVICES - t, SEQ_DEVICES)

    barrier = pltpu.get_barrier_semaphore()
    for t in range(1, SEQ_DEVICES):
        pl.semaphore_signal(barrier, inc=1, device_id=(ahead(t), res), device_id_type=MESH)

    swap[...] = swap_matrix()
    wt[0:256, :] = flip(wq[...])
    wt[256:512, :] = flip(wv[...])
    wt[512:768, :] = flip(wg[...])
    wide[...] = jnp.zeros_like(wide)

    @pl.loop(0, 8)
    def _(g):
        rows = pl.ds(pl.multiple_of(g * 256, 256), 256)
        turned = matmul(swap[...], xc[rows, :]).astype(BF16)
        for r in range(16):
            x2[pl.ds(pl.multiple_of(r * 128 + g * 16, 16), 16), :] = turned[16 * r : 16 * r + 16, :]

    pl.semaphore_wait(barrier, SEQ_DEVICES - 1)
    scale = 1.0 / math.sqrt(HEAD_DIM)

    def result(block, t):
        g = ahead(t)
        return remote(
            done.at[pl.ds(block * 4, 4), pl.ds(pl.multiple_of(g * 16, 16), 16), :],
            back.at[pl.ds(me * 16 + block * 4, 4)],
            send_sem.at[block, t], recv_sem.at[block, t], (g, res),
        )

    @pl.loop(0, 4)
    def _(block):
        rows = pl.ds(pl.multiple_of(block * 512, 512), 512)
        entries = x2[rows, :].astype(F32)
        part = layer_normalize(entries).astype(BF16)
        keys = matmul(part, wk[...]).astype(BF16)
        turned = matmul_nt(wt[...], part)
        queries = turned[0:256, :].astype(BF16)
        values = turned[256:512, :].astype(BF16)
        gate = jax.nn.sigmoid(turned[512:768, :])
        updates = []
        for r in range(4):
            lanes = slice(128 * r, 128 * r + 128)
            for h in range(HEADS):
                wide[r, 32 * h : 32 * h + 32, 128 * h : 128 * h + 128] = queries[
                    32 * h : 32 * h + 32, lanes
                ]
            scores = matmul(keys[lanes, :], wide[r])
            highest = jnp.max(scores, axis=0, keepdims=True)
            expo = jnp.exp((scores - highest) * scale)
            total = jnp.sum(expo, axis=0, keepdims=True)
            weights = (expo * (1.0 / total)).astype(BF16)
            mixed = []
            for h in range(0, HEADS, 2):
                both = matmul(values[32 * h : 32 * h + 64, lanes], weights[:, 128 * h : 128 * h + 256])
                mixed += [both[0:32, 0:128], both[32:64, 128:256]]
            mixed = jnp.concatenate(mixed, axis=0)
            updates.append((gate[:, lanes] * mixed).astype(BF16).astype(F32).T.astype(BF16))
        update = jnp.concatenate(updates, axis=0)
        after = (entries + matmul(update, wf[...])).astype(BF16).astype(F32)
        hidden = matmul(layer_normalize(after).astype(BF16), we[...])
        hidden = jnp.maximum(hidden, 0.0).astype(BF16)
        total = (after + matmul(hidden, ws[...])).astype(BF16)
        for r in range(4):
            done[block * 4 + r] = total[128 * r : 128 * r + 128, :]
        for t in range(1, SEQ_DEVICES):
            result(block, t).start()

    def finish(g, blocks):
        turned = matmul(swap[...], blocks).astype(BF16)
        for s in range(16):
            out[s, pl.ds(pl.multiple_of(g * 16, 16), 16), :] = turned[16 * s : 16 * s + 16, :]

    mine = done[:, pl.ds(pl.multiple_of(me * 16, 16), 16), :]
    finish(me, mine.reshape(256, 256))

    @pl.loop(1, 8)
    def _(t):
        g = behind(t)
        for block in range(4):
            remote(
                done.at[pl.ds(0, 4), pl.ds(0, 16), :],
                back.at[pl.ds(g * 16 + block * 4, 4)],
                send_sem.at[block, t], recv_sem.at[block, t], (ahead(t), res),
            ).wait_recv()
        finish(g, back[pl.ds(g * 16, 16)].reshape(256, 256))

    @pl.loop(1, 8)
    def _(t):
        for block in range(4):
            result(block, t).wait_send()


def column_attention(xc, wq, wk, wv, wg, wf, we, ws):
    vmem = pltpu.VMEM
    return pl.pallas_call(
        column_kernel,
        name="column_attention",
        out_shape=jax.ShapeDtypeStruct((16, 128, 256), BF16),
        in_specs=[pl.BlockSpec(memory_space=vmem)] * 8,
        out_specs=pl.BlockSpec(memory_space=vmem),
        scratch_shapes=[
            vmem((256, 256), BF16),
            vmem((2048, 256), BF16),
            vmem((768, 256), BF16),
            vmem((4, 256, 1024), BF16),
            vmem((16, 128, 256), BF16),
            vmem((128, 16, 256), BF16),
            pltpu.SemaphoreType.DMA((4, 8)),
            pltpu.SemaphoreType.DMA((4, 8)),
        ],
        compiler_params=pltpu.CompilerParams(
            collective_id=1, has_side_effects=True, vmem_limit_bytes=60 * 2**20
        ),
    )(xc, wq, wk, wv, wg, wf, we, ws)


def on_device(
    homolog_tensor,
    horizontal_probe_matrix,
    horizontal_lookup_matrix,
    horizontal_payload_matrix,
    horizontal_sigmoid_matrix,
    horizontal_final_matrix,
    vertical_probe_matrix,
    vertical_lookup_matrix,
    vertical_payload_matrix,
    vertical_sigmoid_matrix,
    vertical_final_matrix,
    expanding_matrix,
    shrinking_matrix,
):
    columns = row_attention(
        homolog_tensor.reshape(2048, 256),
        horizontal_probe_matrix,
        horizontal_lookup_matrix,
        horizontal_payload_matrix,
        horizontal_sigmoid_matrix,
        horizontal_final_matrix,
    )
    return column_attention(
        columns.reshape(2048, 256),
        vertical_probe_matrix,
        vertical_lookup_matrix,
        vertical_payload_matrix,
        vertical_sigmoid_matrix,
        vertical_final_matrix,
        expanding_matrix,
        shrinking_matrix,
    )


def solution(mesh):
    in_specs = (P("seq", "res", None), P(), P(), P(), P(), P(), P(), P(), P(), P(), P(), P(), P())
    out_specs = P("seq", "res", None)
    return jax.shard_map(
        on_device, mesh=mesh, in_specs=in_specs, out_specs=out_specs, check_vma=False
    )
```

time: 580 us -> 180 us (0.31); the launches traced: 570 us -> 179 us
  waiting for transfers between devices: 365 us -> 0 us
  Pallas kernels: 0 us -> 176 us
  matrix products: 67.5 us -> 0 us
  local copies, waits for them, and re-layouts: 52.1 us -> 2.29 us
  blocking collectives: 44.9 us -> 0 us
  other arithmetic: 27 us -> 0 us
  between operations: 13.6 us -> 0.02 us
    all_gather x2 -> x0, waiting for transfers between devices: 184 us -> none  [the longest x1 95.9 us: on_device(): key_piece = lax.all_gather(key_rows, 'res', axis=1, tiled=True)]
    psum x1 -> x0, waiting for transfers between devices: 181 us -> none  [on_device(): tied = lax.psum(partial_logits, 'seq')]
    pallas_call x0 -> x2, Pallas kernels: none -> 176 us  [the longest x1 148 us: row_attention(): pl.pallas_call(row_kernel, name='row_attention', out_shape=jax.ShapeDtype...]
    dot_general x13 -> x0, matrix products: 67.5 us -> none  [the longest x9 20.6 us: linear_project(): return jnp.dot(inputs, weight, preferred_element_type=jnp.float32)]
    all_to_all x2 -> x0, blocking collectives: 44.9 us -> none  [the longest x1 24.1 us: on_device(): lax.all_to_all(blocked, 'seq', split_axis=1, concat_axis=0, tiled=True)]
    reshape x7 -> x0, local copies, waits for them, and re-layouts: 30.2 us -> none  [the longest x1 7.02 us: on_device(): mixed.reshape(total_seqs * count, feature_depth)]
    sub x2 -> x0, other arithmetic: 15.4 us -> none  [softmax_last(): expo = jnp.exp(sample_entries - highest)]
    transpose x2 -> x0, local copies, waits for them, and re-layouts: 9.57 us -> none  [the longest x1 8.37 us: on_device(): jnp.einsum('kmpv,vkml->pkml', weights_col, value_col, preferred_element_t...]
  transfers between devices with their start and end apart: 3 -> 0, of which waited for: 3 -> 0; matrix products, arithmetic and copies ran while one was open for 4% -> 0% of each run, Pallas kernels for 0% -> 0%
where the time goes in v1:
time: 180 us; the launch traced here: 179 us
  Pallas kernels  176 us (98%)
  local copies, waits for them, and re-layouts  2.29 us (1%)
    pallas_call x1, Pallas kernels, row_attention(): pl.pallas_call(row_kernel, name='row_attention', out_shape=jax.ShapeDtype...  148 us
    pallas_call x1, Pallas kernels, column_attention(): pl.pallas_call(column_kernel, name='column_attention', out_shape=jax.Shap...  28.5 us

profile of v1, /device:TPU:0, one launch (start us, length us, event | category | flops | bytes accessed | tf_op | source)
XLA Modules:
  0.0 178.7 jit_solution(1790174096348251705)
XLA Ops:
  0.0 147.9 %row_attention.1 = bf16[128,16,256]{2,1,0:T(8,128)(2,1)} custom-call(bf16[2048,256]{1,0:T(8,128)(2,1)} %bitcast.3, bf16[256,256]{1,0:T(8,128)(2,1)} %wq.2, bf16[256,256]{1,0:T(8,128)(2,1)} %wk.2, bf16[256,256]{1,0:T(8,128)(2,1)} %wv.2, bf16[256,256]{1,0:T(8,128)(2,1)} %wg.2, bf16[256,256]{1,0:T(8,128)(2,1)} %wf.2), custom_call_target="tpu_custom_call" | custom-call | tf_op jit(solution)/shard_map/row_attention/pallas_call | solution.py:435
  147.9 28.5 %column_attention.1 = bf16[16,128,256]{2,1,0:T(8,128)(2,1)} custom-call(bf16[2048,256]{1,0:T(8,128)(2,1)} %bitcast.2, bf16[256,256]{1,0:T(8,128)(2,1)} %wq.3, bf16[256,256]{1,0:T(8,128)(2,1)} %wk.3, bf16[256,256]{1,0:T(8,128)(2,1)} %wv.3, bf16[256,256]{1,0:T(8,128)(2,1)} %wg.3, bf16[256,256]{1,0:T(8,128)(2,1)} %wf.3, bf16[256,1024]{1,0:T(8,128)(2,1)} %we.1, ...), custom_call_target="tpu_custom_call" | custom-call | tf_op jit(solution)/shard_map/column_attention/pallas_call | solution.py:586
  176.4 2.3 %copy.15 = bf16[16,128,256]{2,1,0:T(8,128)(2,1)} copy(bf16[16,128,256]{2,1,0:T(8,128)(2,1)} %column_attention.1) | data formatting | bytes 2097152

commit v2 on v0

v2 whole, which is shorter than its diff:
```python
import math

import jax
import jax.numpy as jnp
from jax import lax
from jax.experimental import pallas as pl
from jax.experimental.pallas import tpu as pltpu
from jax.sharding import PartitionSpec as P

HEADS = 8
HEAD_DIM = 32
SEQ_DEVICES = 8
MESH = pl.DeviceIdType.MESH
BF16 = jnp.bfloat16
F32 = jnp.float32
NT = (((1,), (1,)), ((), ()))


def layer_normalize(entries):
    center = entries - jnp.mean(entries, axis=-1, keepdims=True)
    spread = jnp.mean(center * center, axis=-1, keepdims=True)
    return center * lax.rsqrt(spread + 1e-05)


def matmul(a, b):
    return jnp.dot(a, b, preferred_element_type=F32)


def matmul_nt(a, b):
    return lax.dot_general(a, b, NT, preferred_element_type=F32)


def flip(a):
    return a.astype(F32).T.astype(BF16)


def remote(src, dst, send, recv, device):
    return pltpu.make_async_remote_copy(
        src_ref=src, dst_ref=dst, send_sem=send, recv_sem=recv, device_id=device, device_id_type=MESH
    )


class Exchange:
    def __init__(self, place, src, dst, mid, slot, send, recv, onward_device):
        self.yh, self.xx, self.me, self.res = place
        self.src, self.dst, self.mid, self.slot = src, dst, mid, slot
        self.send, self.recv = send, recv
        self.onward_device = onward_device

    def near(self, k):
        to = self.yh * 4 + lax.rem(self.xx + 4 - k, 4)
        return remote(
            self.src.at[to], self.dst.at[self.slot, self.me],
            self.send.at[0, k], self.recv.at[0, k], (to, self.res),
        )

    def far(self, k):
        column = lax.rem(self.xx + 4 - k, 4)
        return remote(
            self.src.at[(1 - self.yh) * 4 + column], self.mid.at[k],
            self.send.at[1, k], self.recv.at[1, k], (self.yh * 4 + column, self.res),
        )

    def onward(self, k):
        origin = self.yh * 4 + lax.rem(self.xx + k, 4)
        src = self.src.at[(1 - self.yh) * 4 + self.xx] if k == 0 else self.mid.at[k]
        return remote(
            src, self.dst.at[self.slot, origin],
            self.send.at[2, k], self.recv.at[2, k], self.onward_device,
        )

    def start(self):
        for k in (1, 3, 2):
            self.far(k).start()
            self.near(k).start()
        self.onward(0).start()

    def forward(self, k):
        for i in range(1, 4):

            @pl.when(k == i)
            def _(i=i):
                self.far(i).wait_recv()
                self.onward(i).start()

    def arrived(self, place, t):
        @pl.when(t < 4)
        def _():
            remote(
                place, place, self.send.at[0, t], self.recv.at[0, t], self.onward_device
            ).wait_recv()

        @pl.when(t >= 4)
        def _():
            remote(
                place, place, self.send.at[2, t - 4], self.recv.at[2, t - 4], self.onward_device
            ).wait_recv()

    def drain(self):
        for k in range(1, 4):
            self.near(k).wait_send()
            self.far(k).wait_send()
        for k in range(4):
            self.onward(k).wait_send()


def swap_matrix():
    a = lax.broadcasted_iota(jnp.int32, (256, 256), 0)
    b = lax.broadcasted_iota(jnp.int32, (256, 256), 1)
    return jnp.where(b == ((a & 15) << 4) + (a >> 4), 1.0, 0.0).astype(BF16)


def pick_matrix(block, quarter):
    k = lax.broadcasted_iota(jnp.int32, (256, 256), 0) + block * 256
    n = lax.broadcasted_iota(jnp.int32, (256, 256), 1)
    same = ((k >> 7) == (n >> 5)) & (((k >> 5) & 3) == quarter) & ((k & 31) == (n & 31))
    return jnp.where(same, 1.0, 0.0).astype(BF16)


def kernel(
    x, wq, wk, wv, wg, wf, cq, ck, cv, cg, cf, ce, cs, out,
    normed, wt, ks, qs, vs, kmid, qmid, vmid, kz, vz, qg, logits, probs, stats,
    o_part, oc_s, oc_r, oy_s, oy_r, oa_s, oh, xc, gates, picks, osc,
    swap, x2, wide, done, back,
    ka_s, ka_r, qa_s, qa_r, va_s, va_r, kz_s, kz_r, vz_s, vz_r, qp_s, qp_r,
    st_s, st_r, oc_ss, oc_rs, oy_ss, oy_rs, oa_ss, oa_rs, col_s, col_r, back_s, back_r, own_s,
):
    me = lax.axis_index("seq")
    res = lax.axis_index("res")
    z = res // 4
    yl = lax.rem(res // 2, 2)
    c = lax.rem(res, 2)
    here = lax.rem(res, 4)
    yh = me // 4
    xx = lax.rem(me, 4)

    def at_res(zz, yy, cc):
        return (me, zz * 4 + yy * 2 + cc)

    z_up = lax.rem(z + 1, 4)
    z_down = lax.rem(z + 3, 4)
    z_far = lax.rem(z + 2, 4)
    up = at_res(z_up, yl, c)
    down = at_res(z_down, yl, c)
    twin = at_res(z, yl, 1 - c)
    beside = at_res(z, 1 - yl, c)
    across = at_res(z, 1 - yl, 1 - c)
    res_beside = z * 4 + (1 - yl) * 2 + c
    opposite = ((1 - yh) * 4 + xx, res)
    here_twin = yl * 2 + (1 - c)
    here_beside = (1 - yl) * 2 + c
    here_across = (1 - yl) * 2 + (1 - c)

    def diagonal(k):
        return ((1 - yh) * 4 + lax.rem(xx + 4 - k, 4), res_beside)

    def ahead(t):
        return lax.rem(yh + t // 4, 2) * 4 + lax.rem(xx + lax.rem(t, 4), 4)

    def turn(t):
        return lax.rem(me + t, SEQ_DEVICES)

    def unturn(t):
        return lax.rem(me + SEQ_DEVICES - t, SEQ_DEVICES)

    barrier = pltpu.get_barrier_semaphore()
    partners = [(turn(t), res) for t in range(1, SEQ_DEVICES)] + [up, down, twin, beside, across]
    partners += [diagonal(k) for k in range(4)]
    for device in partners:
        pl.semaphore_signal(barrier, inc=1, device_id=device, device_id_type=MESH)

    wt[0:256, :] = flip(wk[...])

    @pl.loop(0, 4)
    def _(quad):
        rows = pl.ds(pl.multiple_of(quad * 512, 512), 512)
        entries = x[pl.ds(quad * 4, 4)].reshape(512, 256)
        part = layer_normalize(entries.astype(F32)).astype(BF16)
        normed[rows, :] = part
        keys = matmul_nt(wt[0:256, :], part).astype(BF16)
        for h in range(HEADS):
            for s in range(4):
                place = pl.ds(pl.multiple_of(quad * 128 + 32 * s, 32), 32)
                ks[h, place, :] = keys[32 * h : 32 * h + 32, 128 * s : 128 * s + 128]

    pl.semaphore_wait(barrier, len(partners))

    place = (yh, xx, me, res)
    ka = Exchange(place, ks, kz, kmid, z, ka_s, ka_r, opposite)
    va = Exchange(place, vs, vz, vmid, z, va_s, va_r, opposite)
    qa = Exchange(place, qs, qg, qmid, here, qa_s, qa_r, diagonal(0))

    own_k = pltpu.make_async_copy(ks.at[me], kz.at[z, me], own_s.at[0])
    own_q = pltpu.make_async_copy(qs.at[me], qg.at[here, me], own_s.at[1])
    own_v = pltpu.make_async_copy(vs.at[me], vz.at[z, me], own_s.at[2])
    own_k.start()
    ka.start()

    wt[256:512, :] = flip(wq[...])
    wt[512:768, :] = flip(wv[...])

    def project(quad, first, target):
        rows = pl.ds(pl.multiple_of(quad * 512, 512), 512)
        turned = matmul_nt(wt[first : first + 256, :], normed[rows, :])
        lanes = pl.ds(pl.multiple_of(quad * 128, 128), 128)
        for h in range(HEADS):
            block = turned[32 * h : 32 * h + 32, :]
            stack = jnp.concatenate([block[:, 128 * s : 128 * s + 128] for s in range(4)], axis=0)
            target[h, :, lanes] = stack.T.astype(BF16)

    def ring(buf, send, recv, t):
        g = ahead(t)
        return (
            remote(buf.at[z, g], buf.at[z, g], send.at[0, t], recv.at[0, t], up),
            remote(buf.at[z, g], buf.at[z, g], send.at[1, t], recv.at[1, t], down),
        )

    def ring_arrived(buf, send, recv, t):
        g = ahead(t)
        remote(buf.at[z_down, g], buf.at[z_down, g], send.at[0, t], recv.at[0, t], up).wait_recv()
        remote(buf.at[z_up, g], buf.at[z_up, g], send.at[1, t], recv.at[1, t], down).wait_recv()

    def onward_up(buf, send, recv, t):
        g = ahead(t)
        return remote(buf.at[z_down, g], buf.at[z_down, g], send.at[2, t], recv.at[2, t], up)

    def onward_down(buf, send, recv, t):
        g = ahead(t)
        return remote(buf.at[z_up, g], buf.at[z_up, g], send.at[2, t], recv.at[2, t], down)

    def far_arrived(buf, send, recv, t):
        g = ahead(t)
        remote(buf.at[z_far, g], buf.at[z_far, g], send.at[2, t], recv.at[2, t], up).wait_recv()

    def ring_forward(buf, send, recv, t):
        ring_arrived(buf, send, recv, t)

        @pl.when(lax.rem(t, 2) == 0)
        def _():
            onward_up(buf, send, recv, t).start()

        @pl.when(lax.rem(t, 2) == 1)
        def _():
            onward_down(buf, send, recv, t).start()

    kzs = (kz, kz_s, kz_r)
    vzs = (vz, vz_s, vz_r)

    def first_place(t):
        half = t // 4
        return here * (1 - half) + here_beside * half

    def second_place(t):
        half = t // 4
        return here_beside * (1 - half) + here * half

    def q_twin(t):
        spot = qg.at[first_place(t), ahead(t)]
        return remote(spot, spot, qp_s.at[0, t], qp_r.at[0, t], twin)

    def q_beside(t):
        spot = qg.at[first_place(t), ahead(t)]
        return remote(spot, spot, qp_s.at[1, t], qp_r.at[1, t], beside)

    def q_onward(t):
        spot = qg.at[second_place(t), ahead(t)]
        return remote(spot, spot, qp_s.at[2, t], qp_r.at[2, t], twin)

    def q_peers(t):
        @pl.when(t == 0)
        def _():
            own_q.wait()

        @pl.when(t > 0)
        def _():
            qa.arrived(qg.at[first_place(t), ahead(t)], t)

        q_beside(t).start()
        q_twin(t).start()

    def q_forward(t):
        spot = qg.at[second_place(t), ahead(t)]
        remote(spot, spot, qp_s.at[1, t], qp_r.at[1, t], beside).wait_recv()
        q_onward(t).start()

    def q_arrived(t):
        half = t // 4
        spot = qg.at[here_twin * (1 - half) + here_across * half, ahead(t)]
        remote(spot, spot, qp_s.at[0, t], qp_r.at[0, t], twin).wait_recv()
        spot = qg.at[here_across * (1 - half) + here_twin * half, ahead(t)]
        remote(spot, spot, qp_s.at[2, t], qp_r.at[2, t], twin).wait_recv()

    def add_chunk(t):
        far_arrived(*kzs, t)
        q_arrived(t)
        g = ahead(t)
        keys = jnp.concatenate([kz[zz, g] for zz in range(4)], axis=1)
        for p in range(4):
            rows = slice(128 * p, 128 * p + 128)
            term = matmul(qg[p, g], keys)

            @pl.when(t == 0)
            def _():
                logits[rows, :] = term

            @pl.when(t > 0)
            def _():
                logits[rows, :] += term

    scale = 1.0 / math.sqrt(SEQ_DEVICES * 16 * HEAD_DIM)

    def stat_copy(i, device):
        return remote(stats.at[here], stats.at[here], st_s.at[i], st_r.at[i], device)

    def stat_wait(i, spot):
        remote(stats.at[spot], stats.at[spot], st_s.at[i], st_r.at[i], twin).wait_recv()

    def local_softmax():
        for p in range(4):
            rows = slice(128 * p, 128 * p + 128)
            highest = jnp.max(logits[rows, :], axis=1, keepdims=True)
            expo = jnp.exp((logits[rows, :] - highest) * scale)
            logits[rows, :] = expo
            total = jnp.sum(expo, axis=1, keepdims=True)
            stats[here, 0, :, rows] = jnp.broadcast_to(highest, (128, 128)).T[0:8, :]
            stats[here, 1, :, rows] = jnp.broadcast_to(total, (128, 128)).T[0:8, :]
        stat_copy(1, beside).start()
        stat_copy(2, across).start()
        stat_copy(0, twin).start()

    def finish_softmax():
        stat_wait(0, here_twin)
        stat_wait(1, here_beside)
        stat_wait(2, here_across)
        highest = stats[0, 0]
        for p in range(1, 4):
            highest = jnp.maximum(highest, stats[p, 0])
        total = jnp.zeros((8, 512), F32)
        for p in range(4):
            total += stats[p, 1] * jnp.exp((stats[p, 0] - highest) * scale)
        factor = jnp.exp((stats[here, 0] - highest) * scale) / total
        for p in range(4):
            rows = slice(128 * p, 128 * p + 128)
            column = jnp.broadcast_to(factor[0:1, rows], (128, 128)).T
            for q in range(4):
                lanes = slice(128 * q, 128 * q + 128)
                probs[rows, lanes] = (logits[rows, lanes] * column).astype(BF16)

    def oc(t):
        return remote(oc_s.at[t], oc_r.at[t], oc_ss.at[t], oc_rs.at[t], twin)

    def oy(t):
        return remote(oy_s.at[t], oy_r.at[t], oy_ss.at[t], oy_rs.at[t], beside)

    def attend(t):
        far_arrived(*vzs, t)
        g = ahead(t)
        slot = lax.rem(t, 2)
        values = jnp.concatenate([vz[zz, g] for zz in range(4)], axis=0)
        for p in range(4):
            o_part[slot, p] = matmul(probs[128 * p : 128 * p + 128, :], values)
        for y in range(2):
            oc_s[t, y] = o_part[slot, 2 * y + 1 - c].astype(BF16)
        oc(t).start()

    same = pl.ds(pl.multiple_of(yh * 64, 64), 64)
    other = pl.ds(pl.multiple_of((1 - yh) * 64, 64), 64)

    def add_twin(t):
        slot = lax.rem(t, 2)
        oc(t).wait_recv()
        oy_s[t, 0] = (o_part[slot, here, other, :] + oc_r[t, yl, other, :].astype(F32)).astype(BF16)
        oy_s[t, 1] = (o_part[slot, here_beside, same, :] + oc_r[t, 1 - yl, same, :].astype(F32)).astype(BF16)
        oy(t).start()

    def oa_near(t, k):
        column = lax.rem(xx + 4 - k, 4)
        return remote(
            oa_s.at[t, 0, pl.ds(pl.multiple_of(column * 16, 16), 16), :], oh.at[me, ahead(t)],
            oa_ss.at[t, k], oa_rs.at[t, k], (yh * 4 + column, res),
        )

    def oa_far(t, k):
        column = lax.rem(xx + 4 - k, 4)
        return remote(
            oa_s.at[t, 1, pl.ds(pl.multiple_of(column * 16, 16), 16), :], oh.at[me, ahead(t)],
            oa_ss.at[t, 4 + k], oa_rs.at[t, 4 + k], diagonal(k),
        )

    def oa_wait(t, k):
        for far in (0, 1):
            if k == 0 and far == 0:
                continue
            yhs = lax.rem(yh + far, 2)
            xs = lax.rem(xx + k, 4)
            g = lax.rem(yhs + t // 4, 2) * 4 + lax.rem(xs + lax.rem(t, 4), 4)
            spot = oh.at[yhs * 4 + xs, g]
            remote(spot, spot, oa_ss.at[t, 4 * far + k], oa_rs.at[t, 4 * far + k], beside).wait_recv()

    def add_beside(t):
        slot = lax.rem(t, 2)
        oy(t).wait_recv()
        oa_s[t, 1] = (
            o_part[slot, here_beside, other, :]
            + oc_r[t, 1 - yl, other, :].astype(F32)
            + oy_r[t, 0].astype(F32)
        ).astype(BF16)
        for k in (2, 1, 3, 0):
            oa_far(t, k).start()
        oa_s[t, 0] = (
            o_part[slot, here, same, :]
            + oc_r[t, yl, same, :].astype(F32)
            + oy_r[t, 1].astype(F32)
        ).astype(BF16)
        for k in (2, 1, 3):
            oa_near(t, k).start()
        oh[me, ahead(t)] = oa_s[t, 0, pl.ds(pl.multiple_of(xx * 16, 16), 16), :]

    mine = pl.ds(pl.multiple_of(me * 16, 16), 16)
    own_x = pltpu.make_async_copy(x.at[:, mine, :], xc.at[mine], own_s.at[3])

    def x_copy(t):
        g = turn(t)
        return remote(
            x.at[:, pl.ds(pl.multiple_of(g * 16, 16), 16), :], xc.at[mine],
            col_s.at[t], col_r.at[t], (g, res),
        )

    def x_start():
        own_x.start()
        for t in range(1, SEQ_DEVICES):
            x_copy(t).start()

    def x_arrived():
        own_x.wait()
        for t in range(1, SEQ_DEVICES):
            spot = xc.at[pl.ds(pl.multiple_of(unturn(t) * 16, 16), 16)]
            remote(spot, spot, col_s.at[t], col_r.at[t], (turn(t), res)).wait_recv()

    def gate_block(i):
        rows = pl.ds(pl.multiple_of(i * 512, 512), 512)
        entries = xc[pl.ds(pl.multiple_of(i * 32, 32), 32)].reshape(512, 256).astype(F32)
        gates[rows, :] = jax.nn.sigmoid(matmul(layer_normalize(entries).astype(BF16), wg[...]))

    def prepare(i):
        @pl.when(i == 0)
        def _():
            wt[0:256, :] = flip(cq[...])
            swap[...] = swap_matrix()

        @pl.when(i == 1)
        def _():
            wt[256:512, :] = flip(cv[...])
            wt[512:768, :] = flip(cg[...])

        for quarter in range(4):
            picks[quarter, pl.ds(pl.multiple_of(i * 256, 256), 256), :] = pick_matrix(i, quarter)
        wide[i] = jnp.zeros((256, 1024), BF16)

    @pl.loop(0, 4)
    def _(quad):
        project(quad, 256, qs)

    own_q.start()
    qa.start()

    def v_project(t):
        project(t, 512, vs)

        @pl.when(t == 3)
        def _():
            own_v.start()
            va.start()

    def k_own(t):
        @pl.when(t == 0)
        def _():
            own_k.wait()

        @pl.when(t > 0)
        def _():
            ka.arrived(kz.at[z, ahead(t)], t)

        for copy in ring(*kzs, t):
            copy.start()

    def v_own(t):
        @pl.when(t == 0)
        def _():
            own_v.wait()

        @pl.when(t > 0)
        def _():
            va.arrived(vz.at[z, ahead(t)], t)

        for copy in ring(*vzs, t):
            copy.start()

    @pl.loop(0, 23)
    def _(tick):
        def during(first, action, count=8):
            @pl.when((tick >= first) & (tick < first + count))
            def _():
                action(tick - first)

        during(15, add_beside)
        during(14, add_twin)
        during(0, k_own)
        during(0, lambda t: ka.forward(t + 1), 3)
        during(0, v_project, 4)
        during(8, v_own)
        during(2, lambda t: ring_forward(*kzs, t))
        during(10, lambda t: ring_forward(*vzs, t))
        during(2, lambda t: qa.forward(t + 1), 3)
        during(5, lambda t: va.forward(t + 1), 3)
        during(2, q_peers)
        during(3, q_forward)
        during(4, prepare, 4)
        during(8, lambda t: x_start(), 1)
        during(4, add_chunk)
        during(12, lambda t: local_softmax(), 1)
        during(13, lambda t: finish_softmax(), 1)
        during(13, attend)
        during(14, lambda t: x_arrived(), 1)
        during(14, gate_block, 4)

    @pl.loop(0, 8)
    def _(t):
        for k in range(4):
            oa_wait(t, k)

    @pl.loop(0, 4)
    def _(quarter):
        stack = jnp.concatenate(
            [
                jnp.concatenate(
                    [oh[h, :, :, 128 * q : 128 * q + 128].reshape(128, 128) for h in range(HEADS)], axis=1
                )
                for q in range(4)
            ],
            axis=0,
        )
        spread = matmul(stack, picks[quarter]).astype(BF16)
        for q in range(4):
            osc[:, 4 * q + quarter] = spread[128 * q : 128 * q + 128, :].reshape(8, 16, 256)

    @pl.loop(0, 8)
    def _(g):
        rows = pl.ds(pl.multiple_of(g * 256, 256), 256)
        update = (gates[rows, :] * osc[g].reshape(256, 256).astype(F32)).astype(BF16)
        entries = xc[pl.ds(pl.multiple_of(g * 16, 16), 16)].reshape(256, 256).astype(F32)
        after = (entries + matmul(update, wf[...])).astype(BF16)
        turned = matmul(swap[...], after).astype(BF16)
        for r in range(16):
            x2[pl.ds(pl.multiple_of(r * 128 + g * 16, 16), 16), :] = turned[16 * r : 16 * r + 16, :]

    col_scale = 1.0 / math.sqrt(HEAD_DIM)

    def result(block, t):
        g = turn(t)
        return remote(
            done.at[pl.ds(block * 4, 4), pl.ds(pl.multiple_of(g * 16, 16), 16), :],
            back.at[pl.ds(me * 16 + block * 4, 4)],
            back_s.at[block, t], back_r.at[block, t], (g, res),
        )

    @pl.loop(0, 4)
    def _(block):
        rows = pl.ds(pl.multiple_of(block * 512, 512), 512)
        entries = x2[rows, :].astype(F32)
        part = layer_normalize(entries).astype(BF16)
        keys = matmul(part, ck[...]).astype(BF16)
        turned = matmul_nt(wt[...], part)
        queries = turned[0:256, :].astype(BF16)
        values = turned[256:512, :].astype(BF16)
        gate = jax.nn.sigmoid(turned[512:768, :])
        updates = []
        for r in range(4):
            lanes = slice(128 * r, 128 * r + 128)
            for h in range(HEADS):
                wide[r, 32 * h : 32 * h + 32, 128 * h : 128 * h + 128] = queries[
                    32 * h : 32 * h + 32, lanes
                ]
            scores = matmul(keys[lanes, :], wide[r])
            highest = jnp.max(scores, axis=0, keepdims=True)
            expo = jnp.exp((scores - highest) * col_scale)
            total = jnp.sum(expo, axis=0, keepdims=True)
            weights = (expo * (1.0 / total)).astype(BF16)
            mixed = []
            for h in range(0, HEADS, 2):
                both = matmul(values[32 * h : 32 * h + 64, lanes], weights[:, 128 * h : 128 * h + 256])
                mixed += [both[0:32, 0:128], both[32:64, 128:256]]
            mixed = jnp.concatenate(mixed, axis=0)
            updates.append((gate[:, lanes] * mixed).astype(BF16).astype(F32).T.astype(BF16))
        update = jnp.concatenate(updates, axis=0)
        after = (entries + matmul(update, cf[...])).astype(BF16).astype(F32)
        hidden = matmul(layer_normalize(after).astype(BF16), ce[...])
        hidden = jnp.maximum(hidden, 0.0).astype(BF16)
        total = (after + matmul(hidden, cs[...])).astype(BF16)
        for r in range(4):
            done[block * 4 + r] = total[128 * r : 128 * r + 128, :]
        for t in range(1, SEQ_DEVICES):
            result(block, t).start()

    def finish(g, blocks):
        turned = matmul(swap[...], blocks).astype(BF16)
        for s in range(16):
            out[s, pl.ds(pl.multiple_of(g * 16, 16), 16), :] = turned[16 * s : 16 * s + 16, :]

    finish(me, done[:, mine, :].reshape(256, 256))

    @pl.loop(1, 8)
    def _(t):
        g = unturn(t)
        for block in range(4):
            spot = back.at[pl.ds(g * 16 + block * 4, 4)]
            remote(spot, spot, back_s.at[block, t], back_r.at[block, t], (turn(t), res)).wait_recv()
        finish(g, back[pl.ds(g * 16, 16)].reshape(256, 256))

    for exchange in (ka, qa, va):
        exchange.drain()
    stat_copy(0, twin).wait_send()
    stat_copy(1, beside).wait_send()
    stat_copy(2, across).wait_send()

    @pl.loop(0, 8)
    def _(t):
        for buf in (kzs, vzs):
            for copy in ring(*buf, t):
                copy.wait_send()

            @pl.when(lax.rem(t, 2) == 0)
            def _():
                onward_up(*buf, t).wait_send()

            @pl.when(lax.rem(t, 2) == 1)
            def _():
                onward_down(*buf, t).wait_send()

        q_twin(t).wait_send()
        q_beside(t).wait_send()
        q_onward(t).wait_send()
        oc(t).wait_send()
        oy(t).wait_send()
        for k in range(4):
            oa_far(t, k).wait_send()
        for k in range(1, 4):
            oa_near(t, k).wait_send()

        @pl.when(t > 0)
        def _():
            x_copy(t).wait_send()
            for block in range(4):
                result(block, t).wait_send()


def on_device(
    homolog_tensor,
    horizontal_probe_matrix,
    horizontal_lookup_matrix,
    horizontal_payload_matrix,
    horizontal_sigmoid_matrix,
    horizontal_final_matrix,
    vertical_probe_matrix,
    vertical_lookup_matrix,
    vertical_payload_matrix,
    vertical_sigmoid_matrix,
    vertical_final_matrix,
    expanding_matrix,
    shrinking_matrix,
):
    dma = pltpu.SemaphoreType.DMA
    vmem = pltpu.VMEM
    return pl.pallas_call(
        kernel,
        name="msa_block",
        out_shape=jax.ShapeDtypeStruct((16, 128, 256), BF16),
        in_specs=[pl.BlockSpec(memory_space=vmem)] * 13,
        out_specs=pl.BlockSpec(memory_space=vmem),
        scratch_shapes=[
            vmem((2048, 256), BF16),
            vmem((768, 256), BF16),
            vmem((8, 512, 128), BF16),
            vmem((8, 128, 512), BF16),
            vmem((8, 128, 512), BF16),
            vmem((4, 512, 128), BF16),
            vmem((4, 128, 512), BF16),
            vmem((4, 128, 512), BF16),
            vmem((4, 8, 512, 128), BF16),
            vmem((4, 8, 128, 512), BF16),
            vmem((4, 8, 128, 512), BF16),
            vmem((512, 512), F32),
            vmem((512, 512), BF16),
            vmem((4, 2, 8, 512), F32),
            vmem((2, 4, 128, 512), F32),
            vmem((8, 2, 128, 512), BF16),
            vmem((8, 2, 128, 512), BF16),
            vmem((8, 2, 64, 512), BF16),
            vmem((8, 2, 64, 512), BF16),
            vmem((8, 2, 64, 512), BF16),
            vmem((8, 8, 16, 512), BF16),
            vmem((128, 16, 256), BF16),
            vmem((2048, 256), F32),
            vmem((4, 1024, 256), BF16),
            vmem((8, 16, 16, 256), BF16),
            vmem((256, 256), BF16),
            vmem((2048, 256), BF16),
            vmem((4, 256, 1024), BF16),
            vmem((16, 128, 256), BF16),
            vmem((128, 16, 256), BF16),
        ]
        + [dma((3, 4))] * 6
        + [dma((3, 8))] * 6
        + [dma((3,))] * 2
        + [dma((8,))] * 4
        + [dma((8, 8))] * 2
        + [dma((8,))] * 2
        + [dma((4, 8))] * 2
        + [dma((4,))],
        compiler_params=pltpu.CompilerParams(
            collective_id=0, has_side_effects=True, vmem_limit_bytes=62 * 2**20
        ),
    )(
        homolog_tensor,
        horizontal_probe_matrix,
        horizontal_lookup_matrix,
        horizontal_payload_matrix,
        horizontal_sigmoid_matrix,
        horizontal_final_matrix,
        vertical_probe_matrix,
        vertical_lookup_matrix,
        vertical_payload_matrix,
        vertical_sigmoid_matrix,
        vertical_final_matrix,
        expanding_matrix,
        shrinking_matrix,
    )


def solution(mesh):
    in_specs = (P("seq", "res", None), P(), P(), P(), P(), P(), P(), P(), P(), P(), P(), P(), P())
    out_specs = P("seq", "res", None)
    return jax.shard_map(
        on_device, mesh=mesh, in_specs=in_specs, out_specs=out_specs, check_vma=False
    )
```

time: 580 us -> 157 us (0.27); the launches traced: 570 us -> 157 us
  waiting for transfers between devices: 365 us -> 0 us
  Pallas kernels: 0 us -> 155 us
  matrix products: 67.5 us -> 0 us
  local copies, waits for them, and re-layouts: 52.1 us -> 2.29 us
  blocking collectives: 44.9 us -> 0 us
  other arithmetic: 27 us -> 0 us
  between operations: 13.6 us -> 0.01 us
    all_gather x2 -> x0, waiting for transfers between devices: 184 us -> none  [the longest x1 95.9 us: on_device(): key_piece = lax.all_gather(key_rows, 'res', axis=1, tiled=True)]
    psum x1 -> x0, waiting for transfers between devices: 181 us -> none  [on_device(): tied = lax.psum(partial_logits, 'seq')]
    pallas_call x0 -> x1, Pallas kernels: none -> 155 us  [on_device(): pl.pallas_call(kernel, name='msa_block', out_shape=jax.ShapeDtypeStruct((...]
    dot_general x13 -> x0, matrix products: 67.5 us -> none  [the longest x9 20.6 us: linear_project(): return jnp.dot(inputs, weight, preferred_element_type=jnp.float32)]
    all_to_all x2 -> x0, blocking collectives: 44.9 us -> none  [the longest x1 24.1 us: on_device(): lax.all_to_all(blocked, 'seq', split_axis=1, concat_axis=0, tiled=True)]
    reshape x7 -> x0, local copies, waits for them, and re-layouts: 30.2 us -> none  [the longest x1 7.02 us: on_device(): mixed.reshape(total_seqs * count, feature_depth)]
    sub x2 -> x0, other arithmetic: 15.4 us -> none  [softmax_last(): expo = jnp.exp(sample_entries - highest)]
    transpose x2 -> x0, local copies, waits for them, and re-layouts: 9.57 us -> none  [the longest x1 8.37 us: on_device(): jnp.einsum('kmpv,vkml->pkml', weights_col, value_col, preferred_element_t...]
  transfers between devices with their start and end apart: 3 -> 0, of which waited for: 3 -> 0; matrix products, arithmetic and copies ran while one was open for 4% -> 0% of each run, Pallas kernels for 0% -> 0%
where the time goes in v2:
time: 157 us
  Pallas kernels  155 us (99%)
  local copies, waits for them, and re-layouts  2.29 us (1%)
    pallas_call x1, Pallas kernels, on_device(): pl.pallas_call(kernel, name='msa_block', out_shape=jax.ShapeDtypeStruct((...  155 us

profile of v2, /device:TPU:0, one launch (start us, length us, event | category | flops | bytes accessed | tf_op | source)
XLA Modules:
  0.0 157.2 jit_solution(7341589854868648353)
XLA Ops:
  0.0 154.9 %msa_block.1 = bf16[16,128,256]{2,1,0:T(8,128)(2,1)} custom-call(bf16[16,128,256]{2,1,0:T(8,128)(2,1)} %x.1, bf16[256,256]{1,0:T(8,128)(2,1)} %wq.1, bf16[256,256]{1,0:T(8,128)(2,1)} %wk.1, bf16[256,256]{1,0:T(8,128)(2,1)} %wv.1, bf16[256,256]{1,0:T(8,128)(2,1)} %wg.1, bf16[256,256]{1,0:T(8,128)(2,1)} %wf.1, bf16[256,256]{1,0:T(8,128)(2,1)} %cq.1, ...), custom_call_target="tpu_custom_call" | custom-call | tf_op jit(solution)/shard_map/msa_block/pallas_call | solution.py:674
  154.9 2.3 %copy.15 = bf16[16,128,256]{2,1,0:T(8,128)(2,1)} copy(bf16[16,128,256]{2,1,0:T(8,128)(2,1)} %msa_block.1) | data formatting | bytes 2097152

commit v3 on v2

--- a/solution.py
+++ b/solution.py
@@ -50,7 +50,7 @@
     def near(self, k):
         to = self.yh * 4 + lax.rem(self.xx + 4 - k, 4)
         return remote(
-            self.src.at[to], self.dst.at[self.slot, self.me],
+            self.src.at[to], self.dst.at[self.slot, k],
             self.send.at[0, k], self.recv.at[0, k], (to, self.res),
         )
 
@@ -62,39 +62,43 @@
         )
 
     def onward(self, k):
-        origin = self.yh * 4 + lax.rem(self.xx + k, 4)
         src = self.src.at[(1 - self.yh) * 4 + self.xx] if k == 0 else self.mid.at[k]
         return remote(
-            src, self.dst.at[self.slot, origin],
+            src, self.dst.at[self.slot, 4 + k],
             self.send.at[2, k], self.recv.at[2, k], self.onward_device,
         )
 
     def start(self):
         for k in (1, 3, 2):
-            self.far(k).start()
             self.near(k).start()
         self.onward(0).start()
-
-    def forward(self, k):
-        for i in range(1, 4):
-
-            @pl.when(k == i)
-            def _(i=i):
-                self.far(i).wait_recv()
-                self.onward(i).start()
-
-    def arrived(self, place, t):
-        @pl.when(t < 4)
+        for k in (1, 3, 2):
+            self.far(k).start()
+
+    def forward(self):
+        for k in (1, 3, 2):
+            self.far(k).wait_recv()
+            self.onward(k).start()
+
+    def arrived(self, place, pair, own):
+        def wait(leg, k, t):
+            spot = self.dst.at[place, t]
+            remote(spot, spot, self.send.at[leg, k], self.recv.at[leg, k], self.onward_device).wait_recv()
+
+        @pl.when(pair == 0)
         def _():
-            remote(
-                place, place, self.send.at[0, t], self.recv.at[0, t], self.onward_device
-            ).wait_recv()
-
-        @pl.when(t >= 4)
+            own.wait()
+            wait(0, 1, 1)
+
+        @pl.when(pair == 1)
         def _():
-            remote(
-                place, place, self.send.at[2, t - 4], self.recv.at[2, t - 4], self.onward_device
-            ).wait_recv()
+            wait(0, 2, 2)
+            wait(0, 3, 3)
+
+        @pl.when(pair >= 2)
+        def _():
+            wait(2, 2 * pair - 4, 2 * pair)
+            wait(2, 2 * pair - 3, 2 * pair + 1)
 
     def drain(self):
         for k in range(1, 4):
@@ -121,7 +125,7 @@
     x, wq, wk, wv, wg, wf, cq, ck, cv, cg, cf, ce, cs, out,
     normed, wt, ks, qs, vs, kmid, qmid, vmid, kz, vz, qg, logits, probs, stats,
     o_part, oc_s, oc_r, oy_s, oy_r, oa_s, oh, xc, gates, picks, osc,
-    swap, x2, wide, done, back,
+    swap, x2, wide, done,
     ka_s, ka_r, qa_s, qa_r, va_s, va_r, kz_s, kz_r, vz_s, vz_r, qp_s, qp_r,
     st_s, st_r, oc_ss, oc_rs, oy_ss, oy_rs, oa_ss, oa_rs, col_s, col_r, back_s, back_r, own_s,
 ):
@@ -154,8 +158,8 @@
     def diagonal(k):
         return ((1 - yh) * 4 + lax.rem(xx + 4 - k, 4), res_beside)
 
-    def ahead(t):
-        return lax.rem(yh + t // 4, 2) * 4 + lax.rem(xx + lax.rem(t, 4), 4)
+    def pair_of(u):
+        return pl.ds(u * 2, 2)
 
     def turn(t):
         return lax.rem(me + t, SEQ_DEVICES)
@@ -190,9 +194,9 @@
     va = Exchange(place, vs, vz, vmid, z, va_s, va_r, opposite)
     qa = Exchange(place, qs, qg, qmid, here, qa_s, qa_r, diagonal(0))
 
-    own_k = pltpu.make_async_copy(ks.at[me], kz.at[z, me], own_s.at[0])
-    own_q = pltpu.make_async_copy(qs.at[me], qg.at[here, me], own_s.at[1])
-    own_v = pltpu.make_async_copy(vs.at[me], vz.at[z, me], own_s.at[2])
+    own_k = pltpu.make_async_copy(ks.at[me], kz.at[z, 0], own_s.at[0])
+    own_q = pltpu.make_async_copy(qs.at[me], qg.at[here, 0], own_s.at[1])
+    own_v = pltpu.make_async_copy(vs.at[me], vz.at[z, 0], own_s.at[2])
     own_k.start()
     ka.start()
 
@@ -208,102 +212,88 @@
             stack = jnp.concatenate([block[:, 128 * s : 128 * s + 128] for s in range(4)], axis=0)
             target[h, :, lanes] = stack.T.astype(BF16)
 
-    def ring(buf, send, recv, t):
-        g = ahead(t)
+    def ring_copy(buf, send, recv, way, source, device, u):
+        spot = buf.at[source, pair_of(u)]
+        return remote(spot, spot, send.at[way, u], recv.at[way, u], device)
+
+    def ring(buf, send, recv, u):
         return (
-            remote(buf.at[z, g], buf.at[z, g], send.at[0, t], recv.at[0, t], up),
-            remote(buf.at[z, g], buf.at[z, g], send.at[1, t], recv.at[1, t], down),
-        )
-
-    def ring_arrived(buf, send, recv, t):
-        g = ahead(t)
-        remote(buf.at[z_down, g], buf.at[z_down, g], send.at[0, t], recv.at[0, t], up).wait_recv()
-        remote(buf.at[z_up, g], buf.at[z_up, g], send.at[1, t], recv.at[1, t], down).wait_recv()
-
-    def onward_up(buf, send, recv, t):
-        g = ahead(t)
-        return remote(buf.at[z_down, g], buf.at[z_down, g], send.at[2, t], recv.at[2, t], up)
-
-    def onward_down(buf, send, recv, t):
-        g = ahead(t)
-        return remote(buf.at[z_up, g], buf.at[z_up, g], send.at[2, t], recv.at[2, t], down)
-
-    def far_arrived(buf, send, recv, t):
-        g = ahead(t)
-        remote(buf.at[z_far, g], buf.at[z_far, g], send.at[2, t], recv.at[2, t], up).wait_recv()
-
-    def ring_forward(buf, send, recv, t):
-        ring_arrived(buf, send, recv, t)
-
-        @pl.when(lax.rem(t, 2) == 0)
+            ring_copy(buf, send, recv, 0, z, up, u),
+            ring_copy(buf, send, recv, 1, z, down, u),
+        )
+
+    def onward_up(buf, send, recv, u):
+        return ring_copy(buf, send, recv, 2, z_down, up, u)
+
+    def onward_down(buf, send, recv, u):
+        return ring_copy(buf, send, recv, 2, z_up, down, u)
+
+    def far_arrived(buf, send, recv, u):
+        ring_copy(buf, send, recv, 2, z_far, up, u).wait_recv()
+
+    def ring_forward(buf, send, recv, u):
+        @pl.when(lax.rem(u, 2) == 0)
         def _():
-            onward_up(buf, send, recv, t).start()
-
-        @pl.when(lax.rem(t, 2) == 1)
+            ring_copy(buf, send, recv, 0, z_down, up, u).wait_recv()
+            onward_up(buf, send, recv, u).start()
+            ring_copy(buf, send, recv, 1, z_up, down, u).wait_recv()
+
+        @pl.when(lax.rem(u, 2) == 1)
         def _():
-            onward_down(buf, send, recv, t).start()
+            ring_copy(buf, send, recv, 1, z_up, down, u).wait_recv()
+            onward_down(buf, send, recv, u).start()
+            ring_copy(buf, send, recv, 0, z_down, up, u).wait_recv()
 
     kzs = (kz, kz_s, kz_r)
     vzs = (vz, vz_s, vz_r)
 
-    def first_place(t):
-        half = t // 4
+    def first_place(u):
+        half = u // 2
         return here * (1 - half) + here_beside * half
 
-    def second_place(t):
-        half = t // 4
+    def second_place(u):
+        half = u // 2
         return here_beside * (1 - half) + here * half
 
-    def q_twin(t):
-        spot = qg.at[first_place(t), ahead(t)]
-        return remote(spot, spot, qp_s.at[0, t], qp_r.at[0, t], twin)
-
-    def q_beside(t):
-        spot = qg.at[first_place(t), ahead(t)]
-        return remote(spot, spot, qp_s.at[1, t], qp_r.at[1, t], beside)
-
-    def q_onward(t):
-        spot = qg.at[second_place(t), ahead(t)]
-        return remote(spot, spot, qp_s.at[2, t], qp_r.at[2, t], twin)
-
-    def q_peers(t):
-        @pl.when(t == 0)
-        def _():
-            own_q.wait()
-
-        @pl.when(t > 0)
-        def _():
-            qa.arrived(qg.at[first_place(t), ahead(t)], t)
-
-        q_beside(t).start()
-        q_twin(t).start()
-
-    def q_forward(t):
-        spot = qg.at[second_place(t), ahead(t)]
-        remote(spot, spot, qp_s.at[1, t], qp_r.at[1, t], beside).wait_recv()
-        q_onward(t).start()
-
-    def q_arrived(t):
-        half = t // 4
-        spot = qg.at[here_twin * (1 - half) + here_across * half, ahead(t)]
-        remote(spot, spot, qp_s.at[0, t], qp_r.at[0, t], twin).wait_recv()
-        spot = qg.at[here_across * (1 - half) + here_twin * half, ahead(t)]
-        remote(spot, spot, qp_s.at[2, t], qp_r.at[2, t], twin).wait_recv()
-
-    def add_chunk(t):
-        far_arrived(*kzs, t)
-        q_arrived(t)
-        g = ahead(t)
-        keys = jnp.concatenate([kz[zz, g] for zz in range(4)], axis=1)
+    def q_copy(way, place, device, u):
+        spot = qg.at[place, pair_of(u)]
+        return remote(spot, spot, qp_s.at[way, u], qp_r.at[way, u], device)
+
+    def q_twin(u):
+        return q_copy(0, first_place(u), twin, u)
+
+    def q_beside(u):
+        return q_copy(1, first_place(u), beside, u)
+
+    def q_onward(u):
+        return q_copy(2, second_place(u), twin, u)
+
+    def q_peers(u):
+        qa.arrived(first_place(u), u, own_q)
+        q_beside(u).start()
+        q_twin(u).start()
+
+    def q_forward(u):
+        q_copy(1, second_place(u), beside, u).wait_recv()
+        q_onward(u).start()
+
+    def add_chunk(u):
+        far_arrived(*kzs, u)
+        half = u // 2
+        q_copy(0, here_twin * (1 - half) + here_across * half, twin, u).wait_recv()
+        q_copy(2, here_across * (1 - half) + here_twin * half, twin, u).wait_recv()
+        keys = [
+            jnp.concatenate([kz[zz, 2 * u + i] for zz in range(4)], axis=1) for i in range(2)
+        ]
         for p in range(4):
             rows = slice(128 * p, 128 * p + 128)
-            term = matmul(qg[p, g], keys)
-
-            @pl.when(t == 0)
+            term = matmul(qg[p, 2 * u], keys[0]) + matmul(qg[p, 2 * u + 1], keys[1])
+
+            @pl.when(u == 0)
             def _():
                 logits[rows, :] = term
 
-            @pl.when(t > 0)
+            @pl.when(u > 0)
             def _():
                 logits[rows, :] += term
 
@@ -352,69 +342,82 @@
     def oy(t):
         return remote(oy_s.at[t], oy_r.at[t], oy_ss.at[t], oy_rs.at[t], beside)
 
-    def attend(t):
-        far_arrived(*vzs, t)
-        g = ahead(t)
-        slot = lax.rem(t, 2)
-        values = jnp.concatenate([vz[zz, g] for zz in range(4)], axis=0)
-        for p in range(4):
-            o_part[slot, p] = matmul(probs[128 * p : 128 * p + 128, :], values)
-        for y in range(2):
-            oc_s[t, y] = o_part[slot, 2 * y + 1 - c].astype(BF16)
-        oc(t).start()
+    def attend(u):
+        far_arrived(*vzs, u)
+
+        @pl.loop(0, 2)
+        def _(i):
+            t = 2 * u + i
+            slot = lax.rem(t, 4)
+            values = jnp.concatenate([vz[zz, t] for zz in range(4)], axis=0)
+            for p in range(4):
+                o_part[slot, p] = matmul(probs[128 * p : 128 * p + 128, :], values)
+            for y in range(2):
+                oc_s[t, y] = o_part[slot, 2 * y + 1 - c].astype(BF16)
+            oc(t).start()
 
     same = pl.ds(pl.multiple_of(yh * 64, 64), 64)
     other = pl.ds(pl.multiple_of((1 - yh) * 64, 64), 64)
 
-    def add_twin(t):
-        slot = lax.rem(t, 2)
-        oc(t).wait_recv()
-        oy_s[t, 0] = (o_part[slot, here, other, :] + oc_r[t, yl, other, :].astype(F32)).astype(BF16)
-        oy_s[t, 1] = (o_part[slot, here_beside, same, :] + oc_r[t, 1 - yl, same, :].astype(F32)).astype(BF16)
-        oy(t).start()
+    def add_twin(u):
+        @pl.loop(0, 2)
+        def _(i):
+            t = 2 * u + i
+            slot = lax.rem(t, 4)
+            oc(t).wait_recv()
+            oy_s[t, 0] = (
+                o_part[slot, here, other, :] + oc_r[t, yl, other, :].astype(F32)
+            ).astype(BF16)
+            oy_s[t, 1] = (
+                o_part[slot, here_beside, same, :] + oc_r[t, 1 - yl, same, :].astype(F32)
+            ).astype(BF16)
+            oy(t).start()
+
+    def column_rows(k):
+        column = lax.rem(xx + 4 - k, 4)
+        return column, pl.ds(pl.multiple_of(column * 16, 16), 16)
 
     def oa_near(t, k):
-        column = lax.rem(xx + 4 - k, 4)
+        column, rows = column_rows(k)
         return remote(
-            oa_s.at[t, 0, pl.ds(pl.multiple_of(column * 16, 16), 16), :], oh.at[me, ahead(t)],
-            oa_ss.at[t, k], oa_rs.at[t, k], (yh * 4 + column, res),
+            oa_s.at[0, t, rows, :], oh.at[me, t], oa_ss.at[t, k], oa_rs.at[t, k], (yh * 4 + column, res)
         )
 
     def oa_far(t, k):
-        column = lax.rem(xx + 4 - k, 4)
+        rows = column_rows(k)[1]
         return remote(
-            oa_s.at[t, 1, pl.ds(pl.multiple_of(column * 16, 16), 16), :], oh.at[me, ahead(t)],
-            oa_ss.at[t, 4 + k], oa_rs.at[t, 4 + k], diagonal(k),
+            oa_s.at[1, t, rows, :], oh.at[me, t], oa_ss.at[t, 4 + k], oa_rs.at[t, 4 + k], diagonal(k)
         )
 
     def oa_wait(t, k):
         for far in (0, 1):
             if k == 0 and far == 0:
                 continue
-            yhs = lax.rem(yh + far, 2)
-            xs = lax.rem(xx + k, 4)
-            g = lax.rem(yhs + t // 4, 2) * 4 + lax.rem(xs + lax.rem(t, 4), 4)
-            spot = oh.at[yhs * 4 + xs, g]
+            source = lax.rem(yh + far, 2) * 4 + lax.rem(xx + k, 4)
+            spot = oh.at[source, t]
             remote(spot, spot, oa_ss.at[t, 4 * far + k], oa_rs.at[t, 4 * far + k], beside).wait_recv()
 
-    def add_beside(t):
-        slot = lax.rem(t, 2)
-        oy(t).wait_recv()
-        oa_s[t, 1] = (
-            o_part[slot, here_beside, other, :]
-            + oc_r[t, 1 - yl, other, :].astype(F32)
-            + oy_r[t, 0].astype(F32)
-        ).astype(BF16)
-        for k in (2, 1, 3, 0):
-            oa_far(t, k).start()
-        oa_s[t, 0] = (
-            o_part[slot, here, same, :]
-            + oc_r[t, yl, same, :].astype(F32)
-            + oy_r[t, 1].astype(F32)
-        ).astype(BF16)
-        for k in (2, 1, 3):
-            oa_near(t, k).start()
-        oh[me, ahead(t)] = oa_s[t, 0, pl.ds(pl.multiple_of(xx * 16, 16), 16), :]
+    def add_beside(u):
+        @pl.loop(0, 2)
+        def _(i):
+            t = 2 * u + i
+            slot = lax.rem(t, 4)
+            oy(t).wait_recv()
+            oa_s[1, t] = (
+                o_part[slot, here_beside, other, :]
+                + oc_r[t, 1 - yl, other, :].astype(F32)
+                + oy_r[t, 0].astype(F32)
+            ).astype(BF16)
+            for k in (2, 1, 3, 0):
+                oa_far(t, k).start()
+            oa_s[0, t] = (
+                o_part[slot, here, same, :]
+                + oc_r[t, yl, same, :].astype(F32)
+                + oy_r[t, 1].astype(F32)
+            ).astype(BF16)
+            for k in (2, 1, 3):
+                oa_near(t, k).start()
+            oh[me, t] = oa_s[0, t, column_rows(0)[1], :]
 
     mine = pl.ds(pl.multiple_of(me * 16, 16), 16)
     own_x = pltpu.make_async_copy(x.at[:, mine, :], xc.at[mine], own_s.at[3])
@@ -464,77 +467,73 @@
     own_q.start()
     qa.start()
 
-    def v_project(t):
-        project(t, 512, vs)
-
-        @pl.when(t == 3)
+    def v_project(u):
+        project(2 * u, 512, vs)
+        project(2 * u + 1, 512, vs)
+
+        @pl.when(u == 1)
         def _():
             own_v.start()
             va.start()
 
-    def k_own(t):
-        @pl.when(t == 0)
-        def _():
-            own_k.wait()
-
-        @pl.when(t > 0)
-        def _():
-            ka.arrived(kz.at[z, ahead(t)], t)
-
-        for copy in ring(*kzs, t):
+    def k_own(u):
+        ka.arrived(z, u, own_k)
+        for copy in ring(*kzs, u):
             copy.start()
 
-    def v_own(t):
-        @pl.when(t == 0)
-        def _():
-            own_v.wait()
-
-        @pl.when(t > 0)
-        def _():
-            va.arrived(vz.at[z, ahead(t)], t)
-
-        for copy in ring(*vzs, t):
+    def v_own(u):
+        va.arrived(z, u, own_v)
+        for copy in ring(*vzs, u):
             copy.start()
 
-    @pl.loop(0, 23)
+    @pl.loop(0, 13)
     def _(tick):
-        def during(first, action, count=8):
+        def during(first, action, count=4):
             @pl.when((tick >= first) & (tick < first + count))
             def _():
                 action(tick - first)
 
-        during(15, add_beside)
-        during(14, add_twin)
+        during(9, add_beside)
+        during(8, add_twin)
         during(0, k_own)
-        during(0, lambda t: ka.forward(t + 1), 3)
-        during(0, v_project, 4)
-        during(8, v_own)
-        during(2, lambda t: ring_forward(*kzs, t))
-        during(10, lambda t: ring_forward(*vzs, t))
-        during(2, lambda t: qa.forward(t + 1), 3)
-        during(5, lambda t: va.forward(t + 1), 3)
-        during(2, q_peers)
-        during(3, q_forward)
-        during(4, prepare, 4)
-        during(8, lambda t: x_start(), 1)
-        during(4, add_chunk)
-        during(12, lambda t: local_softmax(), 1)
-        during(13, lambda t: finish_softmax(), 1)
-        during(13, attend)
-        during(14, lambda t: x_arrived(), 1)
-        during(14, gate_block, 4)
+        during(1, lambda u: ka.forward(), 1)
+        during(1, v_project, 2)
+        during(3, v_own)
+        during(1, lambda u: ring_forward(*kzs, u))
+        during(5, lambda u: ring_forward(*vzs, u))
+        during(2, lambda u: qa.forward(), 1)
+        during(4, lambda u: va.forward(), 1)
+        during(1, q_peers)
+        during(2, q_forward)
+        during(2, prepare, 4)
+        during(7, lambda u: x_start(), 1)
+        during(3, add_chunk)
+        during(6, lambda u: local_softmax(), 1)
+        during(7, lambda u: finish_softmax(), 1)
+        during(7, attend)
+        during(9, lambda u: x_arrived(), 1)
+        during(9, gate_block, 4)
 
     @pl.loop(0, 8)
     def _(t):
         for k in range(4):
             oa_wait(t, k)
+
+    def chunk_of(h, g):
+        return (g // 4 - h // 4) % 2 * 4 + (g - h) % 4
 
     @pl.loop(0, 4)
     def _(quarter):
         stack = jnp.concatenate(
             [
                 jnp.concatenate(
-                    [oh[h, :, :, 128 * q : 128 * q + 128].reshape(128, 128) for h in range(HEADS)], axis=1
+                    [
+                        jnp.concatenate(
+                            [oh[h, chunk_of(h, g), :, 128 * q : 128 * q + 128] for g in range(8)], axis=0
+                        )
+                        for h in range(HEADS)
+                    ],
+                    axis=1,
                 )
                 for q in range(4)
             ],
@@ -544,7 +543,7 @@
         for q in range(4):
             osc[:, 4 * q + quarter] = spread[128 * q : 128 * q + 128, :].reshape(8, 16, 256)
 
-    @pl.loop(0, 8)
+    @pl.loop(0, 8, unroll=4)
     def _(g):
         rows = pl.ds(pl.multiple_of(g * 256, 256), 256)
         update = (gates[rows, :] * osc[g].reshape(256, 256).astype(F32)).astype(BF16)
@@ -560,7 +559,7 @@
         g = turn(t)
         return remote(
             done.at[pl.ds(block * 4, 4), pl.ds(pl.multiple_of(g * 16, 16), 16), :],
-            back.at[pl.ds(me * 16 + block * 4, 4)],
+            out.at[pl.ds(me * 16 + block * 4, 4)],
             back_s.at[block, t], back_r.at[block, t], (g, res),
         )
 
@@ -602,20 +601,7 @@
         for t in range(1, SEQ_DEVICES):
             result(block, t).start()
 
-    def finish(g, blocks):
-        turned = matmul(swap[...], blocks).astype(BF16)
-        for s in range(16):
-            out[s, pl.ds(pl.multiple_of(g * 16, 16), 16), :] = turned[16 * s : 16 * s + 16, :]
-
-    finish(me, done[:, mine, :].reshape(256, 256))
-
-    @pl.loop(1, 8)
-    def _(t):
-        g = unturn(t)
-        for block in range(4):
-            spot = back.at[pl.ds(g * 16 + block * 4, 4)]
-            remote(spot, spot, back_s.at[block, t], back_r.at[block, t], (turn(t), res)).wait_recv()
-        finish(g, back[pl.ds(g * 16, 16)].reshape(256, 256))
+    out[pl.ds(pl.multiple_of(me * 16, 16), 16)] = done[:, mine, :]
 
     for exchange in (ka, qa, va):
         exchange.drain()
@@ -623,23 +609,26 @@
     stat_copy(1, beside).wait_send()
     stat_copy(2, across).wait_send()
 
+    @pl.loop(0, 4)
+    def _(u):
+        for buf in (kzs, vzs):
+            for copy in ring(*buf, u):
+                copy.wait_send()
+
+            @pl.when(lax.rem(u, 2) == 0)
+            def _():
+                onward_up(*buf, u).wait_send()
+
+            @pl.when(lax.rem(u, 2) == 1)
+            def _():
+                onward_down(*buf, u).wait_send()
+
+        q_twin(u).wait_send()
+        q_beside(u).wait_send()
+        q_onward(u).wait_send()
+
     @pl.loop(0, 8)
     def _(t):
-        for buf in (kzs, vzs):
-            for copy in ring(*buf, t):
-                copy.wait_send()
-
-            @pl.when(lax.rem(t, 2) == 0)
-            def _():
-                onward_up(*buf, t).wait_send()
-
-            @pl.when(lax.rem(t, 2) == 1)
-            def _():
-                onward_down(*buf, t).wait_send()
-
-        q_twin(t).wait_send()
-        q_beside(t).wait_send()
-        q_onward(t).wait_send()
         oc(t).wait_send()
         oy(t).wait_send()
         for k in range(4):
@@ -647,11 +636,20 @@
         for k in range(1, 4):
             oa_near(t, k).wait_send()
 
-        @pl.when(t > 0)
-        def _():
-            x_copy(t).wait_send()
-            for block in range(4):
-                result(block, t).wait_send()
+    for t in range(1, SEQ_DEVICES):
+        x_copy(t).wait_send()
+
+    @pl.loop(1, 8)
+    def _(t):
+        g = unturn(t)
+        for block in range(4):
+            spot = out.at[pl.ds(g * 16 + block * 4, 4)]
+            remote(spot, spot, back_s.at[block, t], back_r.at[block, t], (turn(t), res)).wait_recv()
+
+    @pl.loop(1, 8)
+    def _(t):
+        for block in range(4):
+            result(block, t).wait_send()
 
 
 def on_device(
@@ -671,10 +669,10 @@
 ):
     dma = pltpu.SemaphoreType.DMA
     vmem = pltpu.VMEM
-    return pl.pallas_call(
+    columns = pl.pallas_call(
         kernel,
         name="msa_block",
-        out_shape=jax.ShapeDtypeStruct((16, 128, 256), BF16),
+        out_shape=jax.ShapeDtypeStruct((128, 16, 256), BF16),
         in_specs=[pl.BlockSpec(memory_space=vmem)] * 13,
         out_specs=pl.BlockSpec(memory_space=vmem),
         scratch_shapes=[
@@ -692,12 +690,12 @@
             vmem((512, 512), F32),
             vmem((512, 512), BF16),
             vmem((4, 2, 8, 512), F32),
-            vmem((2, 4, 128, 512), F32),
+            vmem((4, 4, 128, 512), F32),
             vmem((8, 2, 128, 512), BF16),
             vmem((8, 2, 128, 512), BF16),
             vmem((8, 2, 64, 512), BF16),
             vmem((8, 2, 64, 512), BF16),
-            vmem((8, 2, 64, 512), BF16),
+            vmem((2, 8, 64, 512), BF16),
             vmem((8, 8, 16, 512), BF16),
             vmem((128, 16, 256), BF16),
             vmem((2048, 256), F32),
@@ -707,10 +705,9 @@
             vmem((2048, 256), BF16),
             vmem((4, 256, 1024), BF16),
             vmem((16, 128, 256), BF16),
-            vmem((128, 16, 256), BF16),
         ]
         + [dma((3, 4))] * 6
-        + [dma((3, 8))] * 6
+        + [dma((3, 4))] * 6
         + [dma((3,))] * 2
         + [dma((8,))] * 4
         + [dma((8, 8))] * 2
@@ -735,6 +732,7 @@
         expanding_matrix,
         shrinking_matrix,
     )
+    return jnp.transpose(columns, (1, 0, 2))
 
 
 def solution(mesh):

time: 157 us -> 142 us (0.904)
  Pallas kernels: 155 us -> 140 us
    pallas_call x1, Pallas kernels: 155 us -> 140 us  [on_device(): pl.pallas_call(kernel, name='msa_block', out_shape=jax.ShapeDtypeStruct((...]
    transpose x0 -> x1, local copies, waits for them, and re-layouts: none -> 2.53 us  [on_device(): return jnp.transpose(columns, (1, 0, 2))]
    unnamed x1 -> x0, local copies, waits for them, and re-layouts: 2.29 us -> none
where the time goes in v3:
time: 142 us
  Pallas kernels  140 us (99%)
  local copies, waits for them, and re-layouts  2.53 us (2%)
    pallas_call x1, Pallas kernels, on_device(): pl.pallas_call(kernel, name='msa_block', out_shape=jax.ShapeDtypeStruct((...  140 us

profile of v3, /device:TPU:0, one launch (start us, length us, event | category | flops | bytes accessed | tf_op | source)
XLA Modules:
  0.0 142.1 jit_solution(9169160936576121783)
XLA Ops:
  0.0 139.5 %msa_block.1 = bf16[128,16,256]{2,1,0:T(8,128)(2,1)} custom-call(bf16[16,128,256]{2,1,0:T(8,128)(2,1)} %x.1, bf16[256,256]{1,0:T(8,128)(2,1)} %wq.1, bf16[256,256]{1,0:T(8,128)(2,1)} %wk.1, bf16[256,256]{1,0:T(8,128)(2,1)} %wv.1, bf16[256,256]{1,0:T(8,128)(2,1)} %wg.1, bf16[256,256]{1,0:T(8,128)(2,1)} %wf.1, bf16[256,256]{1,0:T(8,128)(2,1)} %cq.1, ...), custom_call_target="tpu_custom_call" | custom-call | tf_op jit(solution)/shard_map/msa_block/pallas_call | solution.py:672
  139.6 2.5 %copy.14 = bf16[16,128,256]{2,1,0:T(8,128)(2,1)} copy(bf16[16,128,256]{2,0,1:T(8,128)(2,1)} %bitcast.1) | data formatting | bytes 2097152 | tf_op jit(solution)/shard_map/transpose | solution.py:735

commit v4 on v3

--- a/solution.py
+++ b/solution.py
@@ -41,11 +41,11 @@
 
 
 class Exchange:
-    def __init__(self, place, src, dst, mid, slot, send, recv, onward_device):
+    def __init__(self, place, src, dst, mid, slot, send, recv, onward_device, direct):
         self.yh, self.xx, self.me, self.res = place
         self.src, self.dst, self.mid, self.slot = src, dst, mid, slot
         self.send, self.recv = send, recv
-        self.onward_device = onward_device
+        self.onward_device, self.direct = onward_device, direct
 
     def near(self, k):
         to = self.yh * 4 + lax.rem(self.xx + 4 - k, 4)
@@ -62,10 +62,14 @@
         )
 
     def onward(self, k):
-        src = self.src.at[(1 - self.yh) * 4 + self.xx] if k == 0 else self.mid.at[k]
+        column = self.xx
+        src = self.mid.at[k]
+        if k == 0 or self.direct:
+            column = lax.rem(self.xx + 4 - k, 4)
+            src = self.src.at[(1 - self.yh) * 4 + column]
         return remote(
-            src, self.dst.at[self.slot, 4 + k],
-            self.send.at[2, k], self.recv.at[2, k], self.onward_device,
+            src, self.dst.at[self.slot, 4 + k], self.send.at[2, k], self.recv.at[2, k],
+            ((1 - self.yh) * 4 + column, self.onward_device[1]),
         )
 
     def start(self):
@@ -73,10 +77,13 @@
             self.near(k).start()
         self.onward(0).start()
         for k in (1, 3, 2):
-            self.far(k).start()
+            if self.direct:
+                self.onward(k).start()
+            else:
+                self.far(k).start()
 
     def forward(self):
-        for k in (1, 3, 2):
+        for k in () if self.direct else (1, 3, 2):
             self.far(k).wait_recv()
             self.onward(k).start()
 
@@ -103,7 +110,8 @@
     def drain(self):
         for k in range(1, 4):
             self.near(k).wait_send()
-            self.far(k).wait_send()
+            if not self.direct:
+                self.far(k).wait_send()
         for k in range(4):
             self.onward(k).wait_send()
 
@@ -122,12 +130,13 @@
 
 
 def kernel(
-    x, wq, wk, wv, wg, wf, cq, ck, cv, cg, cf, ce, cs, out,
+    x_in, wq_in, wk_in, wv_in, wg_in, wf_in, cq_in, ck_in, cv_in, cg_in, cf_in, ce_in, cs_in, out,
+    x, wq, wk, wv, wg, wf, cq, ck, cv, cg, cf, ce, cs,
     normed, wt, ks, qs, vs, kmid, qmid, vmid, kz, vz, qg, logits, probs, stats,
     o_part, oc_s, oc_r, oy_s, oy_r, oa_s, oh, xc, gates, picks, osc,
     swap, x2, wide, done,
     ka_s, ka_r, qa_s, qa_r, va_s, va_r, kz_s, kz_r, vz_s, vz_r, qp_s, qp_r,
-    st_s, st_r, oc_ss, oc_rs, oy_ss, oy_rs, oa_ss, oa_rs, col_s, col_r, back_s, back_r, own_s,
+    st_s, st_r, oc_ss, oc_rs, oy_ss, oy_rs, oa_ss, oa_rs, col_s, col_r, back_s, back_r, own_s, load_s,
 ):
     me = lax.axis_index("seq")
     res = lax.axis_index("res")
@@ -173,7 +182,20 @@
     for device in partners:
         pl.semaphore_signal(barrier, inc=1, device_id=device, device_id_type=MESH)
 
+    loads = [
+        pltpu.make_async_copy(source, target, load_s.at[i])
+        for i, (source, target) in enumerate(
+            (
+                (x_in, x), (wk_in, wk), (wq_in, wq), (wv_in, wv), (wg_in, wg), (wf_in, wf), (cq_in, cq),
+                (ck_in, ck), (cv_in, cv), (cg_in, cg), (cf_in, cf), (ce_in, ce), (cs_in, cs),
+            )
+        )
+    ]
+    for load in loads:
+        load.start()
+    loads[1].wait()
     wt[0:256, :] = flip(wk[...])
+    loads[0].wait()
 
     @pl.loop(0, 4)
     def _(quad):
@@ -190,9 +212,9 @@
     pl.semaphore_wait(barrier, len(partners))
 
     place = (yh, xx, me, res)
-    ka = Exchange(place, ks, kz, kmid, z, ka_s, ka_r, opposite)
-    va = Exchange(place, vs, vz, vmid, z, va_s, va_r, opposite)
-    qa = Exchange(place, qs, qg, qmid, here, qa_s, qa_r, diagonal(0))
+    ka = Exchange(place, ks, kz, kmid, z, ka_s, ka_r, opposite, True)
+    va = Exchange(place, vs, vz, vmid, z, va_s, va_r, opposite, False)
+    qa = Exchange(place, qs, qg, qmid, here, qa_s, qa_r, diagonal(0), False)
 
     own_k = pltpu.make_async_copy(ks.at[me], kz.at[z, 0], own_s.at[0])
     own_q = pltpu.make_async_copy(qs.at[me], qg.at[here, 0], own_s.at[1])
@@ -200,6 +222,8 @@
     own_k.start()
     ka.start()
 
+    for load in loads[2:]:
+        load.wait()
     wt[256:512, :] = flip(wq[...])
     wt[512:768, :] = flip(wv[...])
 
@@ -493,14 +517,14 @@
             def _():
                 action(tick - first)
 
-        during(9, add_beside)
-        during(8, add_twin)
         during(0, k_own)
         during(1, lambda u: ka.forward(), 1)
         during(1, v_project, 2)
         during(3, v_own)
         during(1, lambda u: ring_forward(*kzs, u))
         during(5, lambda u: ring_forward(*vzs, u))
+        during(9, add_beside)
+        during(8, add_twin)
         during(2, lambda u: qa.forward(), 1)
         during(4, lambda u: va.forward(), 1)
         during(1, q_peers)
@@ -673,9 +697,12 @@
         kernel,
         name="msa_block",
         out_shape=jax.ShapeDtypeStruct((128, 16, 256), BF16),
-        in_specs=[pl.BlockSpec(memory_space=vmem)] * 13,
+        in_specs=[pl.BlockSpec(memory_space=pl.ANY)] * 13,
         out_specs=pl.BlockSpec(memory_space=vmem),
-        scratch_shapes=[
+        scratch_shapes=[vmem((16, 128, 256), BF16)]
+        + [vmem((256, 256), BF16)] * 10
+        + [vmem((256, 1024), BF16), vmem((1024, 256), BF16)]
+        + [
             vmem((2048, 256), BF16),
             vmem((768, 256), BF16),
             vmem((8, 512, 128), BF16),
@@ -713,7 +740,8 @@
         + [dma((8, 8))] * 2
         + [dma((8,))] * 2
         + [dma((4, 8))] * 2
-        + [dma((4,))],
+        + [dma((4,))]
+        + [dma((13,))],
         compiler_params=pltpu.CompilerParams(
             collective_id=0, has_side_effects=True, vmem_limit_bytes=62 * 2**20
         ),

time: 142 us -> 138 us (0.972)
  Pallas kernels: 140 us -> 135 us
    pallas_call x1, Pallas kernels: 140 us -> 135 us  [on_device(): pl.pallas_call(kernel, name='msa_block', out_shape=jax.ShapeDtypeStruct((...]
where the time goes in v4:
time: 138 us; the launch traced here: 137 us
  Pallas kernels  135 us (98%)
  local copies, waits for them, and re-layouts  2.53 us (2%)
    pallas_call x1, Pallas kernels, on_device(): pl.pallas_call(kernel, name='msa_block', out_shape=jax.ShapeDtypeStruct((...  135 us

profile of v4, /device:TPU:0, one launch (start us, length us, event | category | flops | bytes accessed | tf_op | source)
XLA Modules:
  0.0 137.5 jit_solution(3101349428360617416)
XLA Ops:
  0.0 134.9 %msa_block.1 = bf16[128,16,256]{2,1,0:T(8,128)(2,1)} custom-call(bf16[16,128,256]{2,1,0:T(8,128)(2,1)} %x_in.1, bf16[256,256]{1,0:T(8,128)(2,1)} %wq_in.1, bf16[256,256]{1,0:T(8,128)(2,1)} %wk_in.1, bf16[256,256]{1,0:T(8,128)(2,1)} %wv_in.1, bf16[256,256]{1,0:T(8,128)(2,1)} %wg_in.1, bf16[256,256]{1,0:T(8,128)(2,1)} %wf_in.1, bf16[256,256]{1,0:T(8,128)(2,1)} %cq_in.1, ...), custom_call_target="tpu_custom_call" | custom-call | tf_op jit(solution)/shard_map/msa_block/pallas_call | solution.py:696
  134.9 2.5 %copy.14 = bf16[16,128,256]{2,1,0:T(8,128)(2,1)} copy(bf16[16,128,256]{2,0,1:T(8,128)(2,1)} %bitcast.1) | data formatting | bytes 2097152 | tf_op jit(solution)/shard_map/transpose | solution.py:763

commit v5 on v4

--- a/solution.py
+++ b/solution.py
@@ -372,7 +372,7 @@
         @pl.loop(0, 2)
         def _(i):
             t = 2 * u + i
-            slot = lax.rem(t, 4)
+            slot = t
             values = jnp.concatenate([vz[zz, t] for zz in range(4)], axis=0)
             for p in range(4):
                 o_part[slot, p] = matmul(probs[128 * p : 128 * p + 128, :], values)
@@ -387,7 +387,7 @@
         @pl.loop(0, 2)
         def _(i):
             t = 2 * u + i
-            slot = lax.rem(t, 4)
+            slot = t
             oc(t).wait_recv()
             oy_s[t, 0] = (
                 o_part[slot, here, other, :] + oc_r[t, yl, other, :].astype(F32)
@@ -425,7 +425,7 @@
         @pl.loop(0, 2)
         def _(i):
             t = 2 * u + i
-            slot = lax.rem(t, 4)
+            slot = t
             oy(t).wait_recv()
             oa_s[1, t] = (
                 o_part[slot, here_beside, other, :]
@@ -523,18 +523,18 @@
         during(3, v_own)
         during(1, lambda u: ring_forward(*kzs, u))
         during(5, lambda u: ring_forward(*vzs, u))
-        during(9, add_beside)
-        during(8, add_twin)
         during(2, lambda u: qa.forward(), 1)
         during(4, lambda u: va.forward(), 1)
         during(1, q_peers)
         during(2, q_forward)
         during(2, prepare, 4)
-        during(7, lambda u: x_start(), 1)
+        during(6, lambda u: x_start(), 1)
         during(3, add_chunk)
         during(6, lambda u: local_softmax(), 1)
         during(7, lambda u: finish_softmax(), 1)
+        during(8, add_twin)
         during(7, attend)
+        during(9, add_beside)
         during(9, lambda u: x_arrived(), 1)
         during(9, gate_block, 4)
 
@@ -717,7 +717,7 @@
             vmem((512, 512), F32),
             vmem((512, 512), BF16),
             vmem((4, 2, 8, 512), F32),
-            vmem((4, 4, 128, 512), F32),
+            vmem((8, 4, 128, 512), F32),
             vmem((8, 2, 128, 512), BF16),
             vmem((8, 2, 128, 512), BF16),
             vmem((8, 2, 64, 512), BF16),

time: 138 us -> 135 us (0.978)
  Pallas kernels: 135 us -> 132 us
    pallas_call x1, Pallas kernels: 135 us -> 132 us  [on_device(): pl.pallas_call(kernel, name='msa_block', out_shape=jax.ShapeDtypeStruct((...]
where the time goes in v5:
time: 135 us
  Pallas kernels  132 us (98%)
  local copies, waits for them, and re-layouts  2.53 us (2%)
    pallas_call x1, Pallas kernels, on_device(): pl.pallas_call(kernel, name='msa_block', out_shape=jax.ShapeDtypeStruct((...  132 us

profile of v5, /device:TPU:0, one launch (start us, length us, event | category | flops | bytes accessed | tf_op | source)
XLA Modules:
  0.0 134.5 jit_solution(1758147671578276242)
XLA Ops:
  0.0 132.0 %msa_block.1 = bf16[128,16,256]{2,1,0:T(8,128)(2,1)} custom-call(bf16[16,128,256]{2,1,0:T(8,128)(2,1)} %x_in.1, bf16[256,256]{1,0:T(8,128)(2,1)} %wq_in.1, bf16[256,256]{1,0:T(8,128)(2,1)} %wk_in.1, bf16[256,256]{1,0:T(8,128)(2,1)} %wv_in.1, bf16[256,256]{1,0:T(8,128)(2,1)} %wg_in.1, bf16[256,256]{1,0:T(8,128)(2,1)} %wf_in.1, bf16[256,256]{1,0:T(8,128)(2,1)} %cq_in.1, ...), custom_call_target="tpu_custom_call" | custom-call | tf_op jit(solution)/shard_map/msa_block/pallas_call | solution.py:696
  132.0 2.5 %copy.14 = bf16[16,128,256]{2,1,0:T(8,128)(2,1)} copy(bf16[16,128,256]{2,0,1:T(8,128)(2,1)} %bitcast.1) | data formatting | bytes 2097152 | tf_op jit(solution)/shard_map/transpose | solution.py:763

commit v6 on v5

--- a/solution.py
+++ b/solution.py
@@ -132,7 +132,7 @@
 def kernel(
     x_in, wq_in, wk_in, wv_in, wg_in, wf_in, cq_in, ck_in, cv_in, cg_in, cf_in, ce_in, cs_in, out,
     x, wq, wk, wv, wg, wf, cq, ck, cv, cg, cf, ce, cs,
-    normed, wt, ks, qs, vs, kmid, qmid, vmid, kz, vz, qg, logits, probs, stats,
+    normed, wt, ks, qs, vs, kmid, qmid, vmid, kz, vz, qg, logits, probs, stats, factors,
     o_part, oc_s, oc_r, oy_s, oy_r, oa_s, oh, xc, gates, picks, osc,
     swap, x2, wide, done,
     ka_s, ka_r, qa_s, qa_r, va_s, va_r, kz_s, kz_r, vz_s, vz_r, qp_s, qp_r,
@@ -334,7 +334,7 @@
             rows = slice(128 * p, 128 * p + 128)
             highest = jnp.max(logits[rows, :], axis=1, keepdims=True)
             expo = jnp.exp((logits[rows, :] - highest) * scale)
-            logits[rows, :] = expo
+            probs[rows, :] = expo.astype(BF16)
             total = jnp.sum(expo, axis=1, keepdims=True)
             stats[here, 0, :, rows] = jnp.broadcast_to(highest, (128, 128)).T[0:8, :]
             stats[here, 1, :, rows] = jnp.broadcast_to(total, (128, 128)).T[0:8, :]
@@ -355,10 +355,11 @@
         factor = jnp.exp((stats[here, 0] - highest) * scale) / total
         for p in range(4):
             rows = slice(128 * p, 128 * p + 128)
-            column = jnp.broadcast_to(factor[0:1, rows], (128, 128)).T
-            for q in range(4):
-                lanes = slice(128 * q, 128 * q + 128)
-                probs[rows, lanes] = (logits[rows, lanes] * column).astype(BF16)
+            factors[p] = jnp.broadcast_to(factor[0:1, rows], (128, 128)).T
+
+    def scaled(slot, p, rows):
+        factor = factors[p, rows, :]
+        return o_part[slot, p, rows, :] * jnp.concatenate([factor] * 4, axis=1)
 
     def oc(t):
         return remote(oc_s.at[t], oc_r.at[t], oc_ss.at[t], oc_rs.at[t], twin)
@@ -376,8 +377,16 @@
             values = jnp.concatenate([vz[zz, t] for zz in range(4)], axis=0)
             for p in range(4):
                 o_part[slot, p] = matmul(probs[128 * p : 128 * p + 128, :], values)
+
+        @pl.when(u == 0)
+        def _():
+            finish_softmax()
+
+        @pl.loop(0, 2)
+        def _(i):
+            t = 2 * u + i
             for y in range(2):
-                oc_s[t, y] = o_part[slot, 2 * y + 1 - c].astype(BF16)
+                oc_s[t, y] = scaled(t, 2 * y + 1 - c, slice(None)).astype(BF16)
             oc(t).start()
 
     same = pl.ds(pl.multiple_of(yh * 64, 64), 64)
@@ -390,10 +399,10 @@
             slot = t
             oc(t).wait_recv()
             oy_s[t, 0] = (
-                o_part[slot, here, other, :] + oc_r[t, yl, other, :].astype(F32)
+                scaled(slot, here, other) + oc_r[t, yl, other, :].astype(F32)
             ).astype(BF16)
             oy_s[t, 1] = (
-                o_part[slot, here_beside, same, :] + oc_r[t, 1 - yl, same, :].astype(F32)
+                scaled(slot, here_beside, same) + oc_r[t, 1 - yl, same, :].astype(F32)
             ).astype(BF16)
             oy(t).start()
 
@@ -428,14 +437,14 @@
             slot = t
             oy(t).wait_recv()
             oa_s[1, t] = (
-                o_part[slot, here_beside, other, :]
+                scaled(slot, here_beside, other)
                 + oc_r[t, 1 - yl, other, :].astype(F32)
                 + oy_r[t, 0].astype(F32)
             ).astype(BF16)
             for k in (2, 1, 3, 0):
                 oa_far(t, k).start()
             oa_s[0, t] = (
-                o_part[slot, here, same, :]
+                scaled(slot, here, same)
                 + oc_r[t, yl, same, :].astype(F32)
                 + oy_r[t, 1].astype(F32)
             ).astype(BF16)
@@ -510,7 +519,7 @@
         for copy in ring(*vzs, u):
             copy.start()
 
-    @pl.loop(0, 13)
+    @pl.loop(0, 12)
     def _(tick):
         def during(first, action, count=4):
             @pl.when((tick >= first) & (tick < first + count))
@@ -531,12 +540,11 @@
         during(6, lambda u: x_start(), 1)
         during(3, add_chunk)
         during(6, lambda u: local_softmax(), 1)
-        during(7, lambda u: finish_softmax(), 1)
-        during(8, add_twin)
-        during(7, attend)
-        during(9, add_beside)
-        during(9, lambda u: x_arrived(), 1)
-        during(9, gate_block, 4)
+        during(7, add_twin)
+        during(6, attend)
+        during(8, add_beside)
+        during(8, lambda u: x_arrived(), 1)
+        during(8, gate_block, 4)
 
     @pl.loop(0, 8)
     def _(t):
@@ -567,7 +575,7 @@
         for q in range(4):
             osc[:, 4 * q + quarter] = spread[128 * q : 128 * q + 128, :].reshape(8, 16, 256)
 
-    @pl.loop(0, 8, unroll=4)
+    @pl.loop(0, 8, unroll=8)
     def _(g):
         rows = pl.ds(pl.multiple_of(g * 256, 256), 256)
         update = (gates[rows, :] * osc[g].reshape(256, 256).astype(F32)).astype(BF16)
@@ -717,6 +725,7 @@
             vmem((512, 512), F32),
             vmem((512, 512), BF16),
             vmem((4, 2, 8, 512), F32),
+            vmem((4, 128, 128), F32),
             vmem((8, 4, 128, 512), F32),
             vmem((8, 2, 128, 512), BF16),
             vmem((8, 2, 128, 512), BF16),

time: 135 us -> 134 us (level)
  no operation moved by 1% of the time
where the time goes in v6:
time: 134 us; the launch traced here: 133 us
  Pallas kernels  131 us (98%)
  local copies, waits for them, and re-layouts  2.53 us (2%)
    pallas_call x1, Pallas kernels, on_device(): pl.pallas_call(kernel, name='msa_block', out_shape=jax.ShapeDtypeStruct((...  131 us

profile of v6, /device:TPU:0, one launch (start us, length us, event | category | flops | bytes accessed | tf_op | source)
XLA Modules:
  0.0 133.5 jit_solution(13690635492503106724)
XLA Ops:
  0.0 130.9 %msa_block.1 = bf16[128,16,256]{2,1,0:T(8,128)(2,1)} custom-call(bf16[16,128,256]{2,1,0:T(8,128)(2,1)} %x_in.1, bf16[256,256]{1,0:T(8,128)(2,1)} %wq_in.1, bf16[256,256]{1,0:T(8,128)(2,1)} %wk_in.1, bf16[256,256]{1,0:T(8,128)(2,1)} %wv_in.1, bf16[256,256]{1,0:T(8,128)(2,1)} %wg_in.1, bf16[256,256]{1,0:T(8,128)(2,1)} %wf_in.1, bf16[256,256]{1,0:T(8,128)(2,1)} %cq_in.1, ...), custom_call_target="tpu_custom_call" | custom-call | tf_op jit(solution)/shard_map/msa_block/pallas_call | solution.py:704
  130.9 2.5 %copy.14 = bf16[16,128,256]{2,1,0:T(8,128)(2,1)} copy(bf16[16,128,256]{2,0,1:T(8,128)(2,1)} %bitcast.1) | data formatting | bytes 2097152 | tf_op jit(solution)/shard_map/transpose | solution.py:772
